TPU v7x, 128 devices: a whole 4x4x4 slice. The times are simulated.
128 devices in a mesh: dp: 8 (over y, x_lo), row: 16 (over z, x_hi, core).
Axes of the slice: x: 4 (x_hi: 2, x_lo: 2; x = x_hi * 2 + x_lo), y: 4, z: 4, core: 2. Of those that a mesh axis runs over, the one named last changes fastest.
Arguments:
- fields: bfloat16 [8, 128, 360, 768], P('dp', 'row'), may hold values from -6 to 6
- cotangent: bfloat16 [8, 128, 360, 768], P('dp', 'row'), may hold values from -6 to 6
- norm_gain: float32 [768], replicated, may hold values from 0.5 to 1.5
- weights: bfloat16 [2, 2, 8, 96, 96], replicated, may hold values from -0.4375 to 0.4375
- biases: float32 [2, 2, 768], replicated, may hold values from -3 to 3
- cutoffs: int32 [16], replicated, may hold values from 44 to 176, as said below
Outputs:
- block_out: bfloat16 [8, 128, 360, 768], P('dp', 'row')
- input_grad: bfloat16 [8, 128, 360, 768], P('dp', 'row')
- weight_grads: float32 [2, 2, 8, 96, 96], replicated
- bias_grads: float32 [2, 2, 768], replicated
- gain_grad: float32 [768], replicated
Inputs may be any that keep to these rules, and one draw needn't show every extreme that they name: `cutoffs`: one cutoff equals 176 and one equals 44.
All inputs are finite; a program needn't handle non-finite values.
Results may differ from a plain program's by a relative error of at most 0.015.
Values may be sent and summed in bfloat16 or wider, within the bound.
No kernel may reach another device: no remote copies, remote signals or barrier semaphores. Data moves between devices by JAX's collectives and lax.ppermute only.
A program may use at most 128 MiB of HBM per device.

v0:
```python
import functools
import math

import jax
import jax.numpy as jnp
import ml_dtypes
import numpy as np
from jax import lax
from jax.experimental import pallas as pl
from jax.experimental.pallas import tpu as pltpu
from jax.sharding import PartitionSpec as P

C = 768
NB = 8
BS = 96
W = 360
KW = 176
H = 128
KH = 16
ENS = 8

ROWS = 8
WB = 8
COLS = KW // WB // 2
UNITS = COLS * KH
GC = C // 2
GB = NB // 2
AXES = ("dp", "row")

norm_eps = 1e-06
gelu_coef = 0.7978845608
cube_coef = 0.044715
bf16 = jnp.bfloat16
f32 = jnp.float32
COST = 0
VMEM_LIMIT = 48 * 1024 * 1024
VMEM_MOST = 62 * 1024 * 1024


def first_wave(col, core):
    return WB * (2 * col + (core + col) % 2)


def long_tables():
    firsts = np.array([[first_wave(col, core) for col in range(COLS)] for core in range(2)])
    ids = firsts[:, :, None] + np.arange(WB)
    angle = ((ids[..., None] * np.arange(W)) % W).astype(np.float64) * (2.0 * math.pi / W)
    forward = np.stack([np.cos(angle), -np.sin(angle)], axis=2).astype(np.float32)
    forward = forward / np.float32(math.sqrt(W))
    factor = np.where(ids == 0, 1.0, 2.0).astype(np.float32)[:, :, None, :, None]
    forward, inverse = (
        table.reshape(2, COLS * 2 * WB, W).astype(ml_dtypes.bfloat16)
        for table in (forward, forward * factor)
    )
    return forward, inverse


def latitude_table():
    modes = np.arange(KH)
    signed = np.where(modes < KH // 2, modes, modes - KH)
    angle = ((signed[:, None] * np.arange(H)) % H).astype(np.float64) * (2.0 * math.pi / H)
    cos = (np.cos(angle) / math.sqrt(H)).astype(np.float32).reshape(KH, H // ROWS, ROWS)
    sin = (np.sin(angle) / math.sqrt(H)).astype(np.float32).reshape(KH, H // ROWS, ROWS)
    mixed = np.stack([np.stack([cos, sin], -1), np.stack([-sin, cos], -1)], 1)
    whole = np.einsum("jprhq,kl->rjpkhql", mixed, np.eye(WB, dtype=np.float32))
    return whole.reshape(H // ROWS, KH * 2 * WB, ROWS * 2 * WB).astype(ml_dtypes.bfloat16)


def place(index):
    dp, row = divmod(index, 16)
    y, x_lo = divmod(dp, 2)
    z, rest = divmod(row, 4)
    x_hi, core = divmod(rest, 2)
    return x_hi * 2 + x_lo, y, z, core


def number(x, y, z, core):
    return (y * 2 + x % 2) * 16 + z * 4 + (x // 2) * 2 + core


def shift(array, dx, name):
    pairs = []
    for index in range(128):
        x, y, z, core = place(index)
        pairs.append((index, number((x + dx) % 4, y, z, core)))
    with jax.named_scope(name):
        return lax.ppermute(array, AXES, pairs)


def onward(array, name):
    pairs = []
    for index in range(128):
        x, y, z, core = place(index)
        pairs.append((index, number(x, y, (z + 1 + 2 * core) % 4, core)))
    with jax.named_scope(name):
        return lax.ppermute(array, AXES, pairs)


def swap(array, name, fx=0, fy=0, fz=0, fc=0):
    pairs = []
    for index in range(128):
        x, y, z, core = place(index)
        pairs.append((index, number(x ^ fx, y ^ fy, z ^ fz, core ^ fc)))
    with jax.named_scope(name):
        return lax.ppermute(array, AXES, pairs)


def call(kernel, name, grid, in_specs, out_specs, out_shape, scratch=(), flops=0, moved=0, limit=None):
    return pl.pallas_call(
        kernel,
        name=name,
        grid_spec=pltpu.PrefetchScalarGridSpec(
            num_scalar_prefetch=3,
            grid=grid,
            in_specs=in_specs,
            out_specs=out_specs,
            scratch_shapes=list(scratch),
        ),
        out_shape=out_shape,
        compiler_params=pltpu.CompilerParams(vmem_limit_bytes=limit or VMEM_LIMIT),
        cost_estimate=pl.CostEstimate(flops=COST*flops, bytes_accessed=COST*moved, transcendentals=0),
    )


def layer_norm(block):
    center = block.astype(f32)
    deviation = center - jnp.mean(center, axis=-1, keepdims=True)
    inverse_std = lax.rsqrt(jnp.mean(deviation * deviation, axis=-1, keepdims=True) + norm_eps)
    return deviation * inverse_std, inverse_std


def dot(left, right):
    return jnp.dot(left, right, preferred_element_type=f32)


def dot_nt(left, right):
    return lax.dot_general(left, right, (((1,), (1,)), ((), ())), preferred_element_type=f32)


def dot_tn(left, right):
    return lax.dot_general(left, right, (((0,), (0,)), ((), ())), preferred_element_type=f32)


def own_table(shape):
    return pl.BlockSpec((1,) + shape, lambda i, info, slots, cuts: (info[2], 0, 0))


def beside_table(shape):
    return pl.BlockSpec((1,) + shape, lambda i, info, slots, cuts: (1 - info[2], 0, 0))


def row_block(*shape):
    zeros = (0,) * (len(shape) - 1)
    return pl.BlockSpec(shape, lambda i, info, slots, cuts: (i,) + zeros)


def fixed(*shape):
    zeros = (0,) * len(shape)
    return pl.BlockSpec(shape, lambda i, info, slots, cuts: zeros)


def lon_forward(scalars, array, table, gain=None):
    step = 4

    def kernel(info, slots, cuts, own_t, beside_t, x, *rest):
        for at in range(step):
            if gain is None:
                own, beside = rest
                rows = x[at]
            else:
                scale, own, beside = rest
                rows = (layer_norm(x[at])[0] * scale[...].reshape(1, C)).astype(bf16)
            own[at] = dot(own_t[0], rows).astype(bf16).reshape(COLS, 2 * WB, C)
            beside[at] = dot(beside_t[0], rows).astype(bf16).reshape(COLS, 2 * WB, C)

    specs = [own_table((KW, W)), beside_table((KW, W)), row_block(step, W, C)]
    operands = [table, table, array]
    if gain is not None:
        specs.append(fixed(C))
        operands.append(gain)
    shape = jax.ShapeDtypeStruct((ROWS, COLS, 2 * WB, C), bf16)
    return call(
        kernel,
        "lon_forward",
        (ROWS // step,),
        specs,
        [row_block(step, COLS, 2 * WB, C)] * 2,
        [shape, shape],
        limit=VMEM_MOST,
        flops=2 * ROWS * 2 * KW * W * C,
        moved=2 * ROWS * C * (W + 2 * KW),
    )(*scalars, *operands)


def lane_block(lanes, *shape):
    zeros = (0,) * len(shape)
    return pl.BlockSpec(shape + (lanes,), lambda i, info, slots, cuts: zeros + (i,))


def lat_tables(shape):
    return [
        pl.BlockSpec((1,) + shape, lambda i, info, slots, cuts: (info[3], 0, 0)),
        pl.BlockSpec((1,) + shape, lambda i, info, slots, cuts: (info[4], 0, 0)),
    ]


LANES = 256


def slot_base(info, step, half, owned):
    return (lax.rem(info[0] + step * info[7], 4) * 2 + lax.rem(info[1] + half, 2)) * owned


def lat_forward(scalars, own, beside, table, owned):
    def kernel(info, slots, cuts, own_t, beside_t, x_own, x_beside, *rest):
        outs, over, units = rest[:8], rest[8], rest[9]
        mix = jnp.concatenate([own_t[0], beside_t[0]], axis=1)
        for col in range(COLS):
            rows = jnp.concatenate(
                [x_own[:, col].reshape(-1, LANES), x_beside[:, col].reshape(-1, LANES)], axis=0
            )
            units[col * KH : (col + 1) * KH] = dot(mix, rows).astype(bf16).reshape(KH, 2 * WB, LANES)
        units[UNITS] = jnp.zeros((2 * WB, LANES), bf16)
        for step in range(4):
            for half in range(2):
                base = slot_base(info, step, half, owned)
                for at in range(owned):
                    outs[step * 2 + half][at] = units[slots[base + at]]

        @pl.when(slots[8 * owned] < UNITS)
        def _():
            for at in range(UNITS - 8 * owned):
                over[at] = units[slots[8 * owned + at]]

    shape = jax.ShapeDtypeStruct((owned, 2 * WB, C), bf16)
    return call(
        kernel,
        "lat_forward",
        (C // LANES,),
        lat_tables((KH * 2 * WB, ROWS * 2 * WB)) + [lane_block(LANES, ROWS, COLS, 2 * WB)] * 2,
        [lane_block(LANES, owned, 2 * WB)] * 8 + [lane_block(LANES, UNITS - 8 * owned, 2 * WB)],
        [shape] * 8 + [jax.ShapeDtypeStruct((UNITS - 8 * owned, 2 * WB, C), bf16)],
        [pltpu.VMEM((UNITS + 1, 2 * WB, LANES), bf16)],
        limit=VMEM_MOST,
        flops=2 * 256 * 256 * C * COLS,
        moved=2 * C * 16 * (UNITS + 8 * owned),
    )(*scalars, table, table, own, beside)


def lat_inverse(scalars, pieces, over, table, owned):
    def kernel(info, slots, cuts, own_t, beside_t, *rest):
        arrived, (over, own, beside, units) = rest[:8], rest[8:]
        units[...] = jnp.zeros(units.shape, bf16)
        for step in range(4):
            for half in range(2):
                base = slot_base(info, step, half, owned)
                for at in range(owned):
                    units[slots[base + at]] = arrived[step * 2 + half][at]

        @pl.when(slots[8 * owned] < UNITS)
        def _():
            for at in range(UNITS - 8 * owned):
                units[slots[8 * owned + at]] = over[at]

        mix = jnp.concatenate([own_t[0], beside_t[0]], axis=0)
        for col in range(COLS):
            rows = dot(mix, units[col * KH : (col + 1) * KH].reshape(-1, LANES)).astype(bf16)
            half = ROWS * 2 * WB
            own[:, col] = rows[:half].reshape(ROWS, 2 * WB, LANES)
            beside[:, col] = rows[half:].reshape(ROWS, 2 * WB, LANES)

    shape = jax.ShapeDtypeStruct((ROWS, COLS, 2 * WB, C), bf16)
    return call(
        kernel,
        "lat_inverse",
        (C // LANES,),
        lat_tables((ROWS * 2 * WB, KH * 2 * WB)) + [lane_block(LANES, owned, 2 * WB)] * 8
        + [lane_block(LANES, UNITS - 8 * owned, 2 * WB)],
        [lane_block(LANES, ROWS, COLS, 2 * WB)] * 2,
        [shape, shape],
        [pltpu.VMEM((UNITS + 1, 2 * WB, LANES), bf16)],
        flops=2 * 256 * 256 * C * COLS,
        moved=2 * C * 16 * (UNITS + 8 * owned),
    )(*scalars, table, table, *pieces, over)


def grid_rows(own_t, beside_t, x_own, x_beside, at):
    own = dot(own_t[0], x_own[at].reshape(KW, C))
    return own + dot(beside_t[0], x_beside[at].reshape(KW, C))


def lon_inverse_fields(scalars, own, beside, table, fields):
    step = 2

    def kernel(info, slots, cuts, own_t, beside_t, x_own, x_beside, x, out):
        for at in range(step):
            grid = grid_rows(own_t, beside_t, x_own, x_beside, at)
            out[at] = (x[at].astype(f32) + grid).astype(bf16)

    return call(
        kernel,
        "lon_inverse_fields",
        (ROWS // step,),
        [own_table((W, KW)), beside_table((W, KW))]
        + [row_block(step, COLS, 2 * WB, C)] * 2
        + [row_block(step, W, C)],
        row_block(step, W, C),
        jax.ShapeDtypeStruct((ROWS, W, C), bf16),
        flops=2 * ROWS * 2 * KW * W * C,
        moved=2 * ROWS * C * (2 * W + 2 * KW),
    )(*scalars, table, table, own, beside, fields)


def lon_inverse_grad(scalars, own, beside, table, fields, cotangent, gain):
    step = 2

    def kernel(info, slots, cuts, own_t, beside_t, x_own, x_beside, x, cot, scale, out):
        for at in range(step):
            grid = grid_rows(own_t, beside_t, x_own, x_beside, at)
            normal, inverse_std = layer_norm(x[at])
            scaled = grid * scale[...].reshape(1, C)
            first = jnp.mean(scaled, axis=-1, keepdims=True)
            second = jnp.mean(scaled * normal, axis=-1, keepdims=True)
            grad = inverse_std * (scaled - first - normal * second)
            out[at] = (cot[at].astype(f32) + grad).astype(bf16)

    return call(
        kernel,
        "lon_inverse_grad",
        (ROWS // step,),
        [own_table((W, KW)), beside_table((W, KW))]
        + [row_block(step, COLS, 2 * WB, C)] * 2
        + [row_block(step, W, C)] * 2
        + [fixed(C)],
        row_block(step, W, C),
        jax.ShapeDtypeStruct((ROWS, W, C), bf16),
        limit=VMEM_MOST,
        flops=2 * ROWS * 2 * KW * W * C,
        moved=2 * ROWS * C * (3 * W + 2 * KW),
    )(*scalars, table, table, own, beside, fields, cotangent, gain)


def wide_weights(scalars, weights):
    def kernel(info, slots, cuts, w, out):
        row = lax.broadcasted_iota(jnp.int32, (BS, GC), 0)
        lane = lax.broadcasted_iota(jnp.int32, (BS, GC), 1)
        for layer in range(2):
            for block in range(GB):
                move = (lane == row + block * BS).astype(f32).astype(bf16)
                real = dot(w[layer, 0, block], move)
                imag = dot(w[layer, 1, block], move)
                top = slice(block * BS, (block + 1) * BS)
                low = slice(GC + block * BS, GC + (block + 1) * BS)
                out[layer, 0, top, :GC] = real.astype(bf16)
                out[layer, 0, top, GC:] = imag.astype(bf16)
                out[layer, 0, low, :GC] = (-imag).astype(bf16)
                out[layer, 0, low, GC:] = real.astype(bf16)

    return call(
        kernel,
        "wide_weights",
        (2,),
        [pl.BlockSpec((2, 2, GB, BS, BS), lambda i, info, slots, cuts: (0, 0, i, 0, 0))],
        pl.BlockSpec((2, 1, C, C), lambda i, info, slots, cuts: (0, i, 0, 0)),
        jax.ShapeDtypeStruct((2, 2, C, C), bf16),
        moved=2 * 5 * C * C,
    )(*scalars, weights)


def gelu_pair(values):
    inner = jnp.tanh(gelu_coef * (values + cube_coef * values * values * values))
    value = 0.5 * values * (1.0 + inner)
    slope = 0.5 * (1.0 + inner) + 0.5 * values * (1.0 - inner * inner) * gelu_coef * (
        1.0 + 3.0 * cube_coef * values * values
    )
    return (value, slope)


def own_first(info, owned):
    return (info[0] * 2 + info[5]) * owned


def kept_of(info, slots, cuts, place):
    unit = slots[place]
    col = lax.div(unit, KH)
    first = WB * (2 * col + lax.rem(info[2] + col, 2))
    return jnp.where(unit < UNITS, cuts[lax.rem(unit, KH)] - first, 0)


def each(count, step):
    if count > 24:
        pl.loop(0, count)(step)
    else:
        for at in range(count):
            step(at)


def unit_rows(at):
    return pl.ds(pl.multiple_of(at * WB, WB) if not isinstance(at, int) else at * WB, WB)


def gather_units(info, slots, cuts, left, right, held, first):
    row = lax.broadcasted_iota(jnp.int32, (WB, GC), 0)

    def step(at):
        unit = left[at].astype(f32)
        if right is not None:
            unit = unit + right[at].astype(f32)
        kept = row < kept_of(info, slots, cuts, first + at)
        held[unit_rows(at), :GC] = jnp.where(kept, unit[:WB], 0.0)
        held[unit_rows(at), GC:] = jnp.where(kept, unit[WB:], 0.0)

    each(left.shape[0], step)
    return held[...].astype(bf16)


def scatter_units(info, slots, cuts, held, out, first):
    row = lax.broadcasted_iota(jnp.int32, (WB, GC), 0)

    def step(at):
        kept = row < kept_of(info, slots, cuts, first + at)
        real = jnp.where(kept, held[unit_rows(at), :GC], 0.0)
        imag = jnp.where(kept, held[unit_rows(at), GC:], 0.0)
        out[at] = jnp.concatenate([real, imag], axis=0).astype(bf16)

    each(out.shape[0], step)


def group_block(rows):
    return pl.BlockSpec((1, rows, C), lambda i, info, slots, cuts: (i, 0, 0))


def weight_block(layer):
    return pl.BlockSpec((1, 1, C, C), lambda i, info, slots, cuts: (layer, i, 0, 0))


def spectral_forward(scalars, units, wide, biases, first=None):
    owned = units[0].shape[0]
    count = owned * WB

    def kernel(info, slots, cuts, xl, *rest):
        xr = rest[0] if len(units) == 2 else None
        w0, w1, bias, out, given, hidden, slope, held = rest[-8:]
        place = own_first(info, owned) if first is None else first
        given[0] = gather_units(info, slots, cuts, xl, xr, held, place)
        b0 = jnp.concatenate([bias[0, 0:1, :], bias[0, 1:2, :]], axis=1)
        b1 = jnp.concatenate([bias[1, 0:1, :], bias[1, 1:2, :]], axis=1)
        act, slope[0] = gelu_pair(dot(given[0], w0[0, 0]) + b0)
        hidden[0] = act.astype(bf16)
        held[...] = dot(hidden[0], w1[0, 0]) + b1
        scatter_units(info, slots, cuts, held, out, place)

    return call(
        kernel,
        "spectral_forward",
        (2,),
        [lane_block(GC, owned, 2 * WB)] * len(units)
        + [weight_block(0), weight_block(1), lane_block(GC, 2, 2)],
        [lane_block(GC, owned, 2 * WB)] + [group_block(count)] * 3,
        [jax.ShapeDtypeStruct((owned, 2 * WB, C), bf16)]
        + [jax.ShapeDtypeStruct((2, count, C), kind) for kind in (bf16, bf16, f32)],
        [pltpu.VMEM((count, C), f32)],
        flops=8 * count * C * C,
        moved=8 * C * C + 20 * count * C,
    )(*scalars, *units, wide, wide, biases)


def spectral_backward(scalars, units, wide, given, slope, first=None):
    owned = units[0].shape[0]
    count = owned * WB

    def kernel(info, slots, cuts, xl, *rest):
        xr = rest[0] if len(units) == 2 else None
        w0, w1, given, slope, out, upper, lower, sums, held = rest[-9:]
        place = own_first(info, owned) if first is None else first
        upper[0] = gather_units(info, slots, cuts, xl, xr, held, place)
        sums[0] = jnp.zeros(sums.shape[1:], f32)
        sums[0, 0:1, :] = jnp.sum(upper[0].astype(f32), axis=0, keepdims=True)
        low = (dot_nt(upper[0], w1[0, 0]) * slope[0]).astype(bf16)
        lower[0] = low
        sums[0, 1:2, :] = jnp.sum(low.astype(f32), axis=0, keepdims=True)
        held[...] = dot_nt(low, w0[0, 0])
        scatter_units(info, slots, cuts, held, out, place)
        sums[0, 2:3, :] = jnp.sum(held[...] * given[0].astype(f32), axis=0, keepdims=True)

    return call(
        kernel,
        "spectral_backward",
        (2,),
        [lane_block(GC, owned, 2 * WB)] * len(units)
        + [weight_block(0), weight_block(1), group_block(count), group_block(count)],
        [lane_block(GC, owned, 2 * WB)] + [group_block(count)] * 2 + [group_block(8)],
        [jax.ShapeDtypeStruct((owned, 2 * WB, C), bf16)]
        + [jax.ShapeDtypeStruct((2, count, C), bf16)] * 2
        + [jax.ShapeDtypeStruct((2, 8, C), f32)],
        [pltpu.VMEM((count, C), f32)],
        flops=8 * count * C * C,
        moved=8 * C * C + 20 * count * C,
    )(*scalars, *units, wide, wide, given, slope)


SHARE = 416
PIECE = SHARE // 4


def weight_sums(scalars, given, lower, hidden, upper, sums, more=None):
    count = given.shape[1]

    def group(rows, lanes=C):
        return pl.BlockSpec(
            (1, rows, lanes), lambda i, info, slots, cuts: (lax.rem(i + 1 + info[2], 2), 0, 0)
        )

    def kernel(info, slots, cuts, u0, y0, u1, y1, small, *rest):
        send, keep, out = rest[-3:]
        lane = lax.div(lax.broadcasted_iota(jnp.int32, (BS, GC), 1), BS)
        for layer, (u, y) in enumerate(((u0, y0), (u1, y1))):
            whole = dot_tn(u[0], y[0])
            real = whole[:GC, :GC] + whole[GC:, GC:]
            imag = whole[:GC, GC:] - whole[GC:, :GC]
            for part, value in enumerate((real, imag)):
                folded = value[:BS]
                for block in range(1, GB):
                    folded = jnp.where(lane == block, value[block * BS : (block + 1) * BS], folded)
                first = (layer * 2 + part) * BS
                out[first : first + BS, :] = folded
        out[4 * BS : 4 * BS + 8, :] = small[0, :, :GC]
        out[4 * BS + 8 : 4 * BS + 16, :] = small[0, :, GC:]
        out[4 * BS + 16 :, :] = jnp.zeros((SHARE - 4 * BS - 16, GC), f32)
        total = out[...]
        if more is not None:
            total = total + rest[0][0]

        @pl.when(pl.program_id(0) == 0)
        def _():
            send[...] = total.astype(send.dtype)

        @pl.when(pl.program_id(0) == 1)
        def _():
            keep[...] = total

    return call(
        kernel,
        "weight_sums",
        (2,),
        [group(count)] * 4 + [group(8)] + ([] if more is None else [group(SHARE, GC)]),
        [fixed(SHARE, GC)] * 2,
        [
            jax.ShapeDtypeStruct((SHARE, GC), f32 if more is None else bf16),
            jax.ShapeDtypeStruct((SHARE, GC), f32),
        ],
        [pltpu.VMEM((SHARE, GC), f32)],
    )(*scalars, given, lower, hidden, upper, sums, *([] if more is None else [more]))


def split_sum(scalars, left, right):
    def kernel(info, slots, cuts, left, right, *outs):
        for far in range(4):
            rows = pl.ds(pl.multiple_of(jnp.bitwise_xor(info[6], far) * PIECE, 8), PIECE)
            outs[far][...] = (left[rows, :] + right[rows, :].astype(f32)).astype(bf16)

    return call(
        kernel,
        "split_sum",
        (1,),
        [fixed(SHARE, GC)] * 2,
        [fixed(PIECE, GC)] * 4,
        [jax.ShapeDtypeStruct((PIECE, GC), bf16)] * 4,
        moved=16 * SHARE * GC,
    )(*scalars, left, right)


def place_sums(scalars, pieces, gain):
    spectral_scale = 1.0 / math.sqrt(ENS * KH * KW)
    gain_scale = 1.0 / math.sqrt(ENS * H * W)

    def kernel(info, slots, cuts, p0, p1, p2, p3, scale, weight_out, bias_out, gain_out, held):
        for far, piece in enumerate((p0, p1, p2, p3)):
            rows = pl.ds(pl.multiple_of(jnp.bitwise_xor(info[6], far) * PIECE, 8), PIECE)
            held[info[2], rows, :] = piece[0].astype(f32)
            held[1 - info[2], rows, :] = piece[1].astype(f32)
        for group in range(2):
            lanes = slice(group * GC, (group + 1) * GC)
            for layer in range(2):
                for part in range(2):
                    first = (layer * 2 + part) * BS
                    value = held[group, first : first + BS, :] * spectral_scale
                    for block in range(GB):
                        weight_out[layer, part, group * GB + block] = value[
                            :, block * BS : (block + 1) * BS
                        ]
                    at = 4 * BS + part * 8 + 1 - layer
                    bias_out[layer, part : part + 1, lanes] = (
                        held[group, at : at + 1, :] * spectral_scale
                    )
            at = 4 * BS + 2
            both = held[group, at : at + 1, :] + held[group, at + 8 : at + 9, :]
            gain_out[lanes] = (both * gain_scale).reshape(GC) / scale[lanes]

    return call(
        kernel,
        "place_sums",
        (1,),
        [fixed(2, PIECE, GC)] * 4 + [fixed(C)],
        [fixed(2, 2, NB, BS, BS), fixed(2, 2, C), fixed(C)],
        [
            jax.ShapeDtypeStruct((2, 2, NB, BS, BS), f32),
            jax.ShapeDtypeStruct((2, 2, C), f32),
            jax.ShapeDtypeStruct((C,), f32),
        ],
        [pltpu.VMEM((2, SHARE, GC), f32)],
        moved=16 * SHARE * GC,
    )(*scalars, *pieces, gain)


def add(*arrays):
    total = arrays[0].astype(f32)
    for array in arrays[1:]:
        total = total + array.astype(f32)
    return total.astype(bf16)


def four(own, first, second, third):
    own, first, second, third = (array.astype(f32) for array in (own, first, second, third))
    return ((own + first) + (second + third)).astype(bf16)


class Order:
    def __init__(self, info, slots, cutoffs):
        self.info, self.rest = info, (slots, cutoffs)

    @property
    def scalars(self):
        return (self.info,) + self.rest

    def ready(self, *arrays):
        return lax.optimization_barrier(arrays + (self.info,))[:-1]

    def wait(self, *arrays):
        *arrays, self.info = lax.optimization_barrier(tuple(arrays) + (self.info,))
        return arrays[0] if len(arrays) == 1 else arrays


def kept_units(cutoffs, core):
    col = jnp.arange(COLS, dtype=jnp.int32)[:, None]
    return (cutoffs[None, :] > first_wave(col, core)).astype(jnp.int32)


def unit_slots(cutoffs, core, total):
    unit = jnp.arange(UNITS, dtype=jnp.int32)[:, None, None]
    col = jnp.arange(COLS, dtype=jnp.int32)[None, :, None]
    mode = jnp.arange(KH, dtype=jnp.int32)[None, None, :]
    kept = kept_units(cutoffs, core)[None]
    rank = jnp.sum(jnp.where(col * KH + mode <= unit, kept, 0), axis=(1, 2))
    place_of = jnp.arange(total, dtype=jnp.int32)
    return jnp.sum((rank[None, :] <= place_of[:, None]).astype(jnp.int32), axis=1)


def past_slots(order, owned, f_over, g_over, wide, biases):
    groups = [[2 * at + core for at in range(8)] for core in range(2)]
    f_sum, g_sum = lax.psum(
        (f_over.astype(f32), g_over.astype(f32)), "row", axis_index_groups=groups
    )
    first = 8 * owned
    shrunk, given, hidden, slope = spectral_forward(
        order.scalars, (f_sum,), wide, biases, first
    )
    bottom, upper, lower, sums = spectral_backward(
        order.scalars, (g_sum,), wide, given, slope, first
    )
    other, own = weight_sums(order.scalars, given, lower, hidden, upper, sums)
    counted = (order.info[0] == 0) & (order.info[1] == 0)
    more = jnp.where(order.info[2] == 0, jnp.stack([own, other]), jnp.stack([other, own]))
    return shrunk, bottom, jnp.where(counted, more, 0.0)


def whole_pass(owned, field_in, grad_out, gain, weights, biases, cutoffs):
    dp = lax.axis_index("dp").astype(jnp.int32)
    row = lax.axis_index("row").astype(jnp.int32)
    z, x_hi, core = row // 4, (row // 2) % 2, row % 2
    y, x_lo = dp // 2, dp % 2
    half_owned = ((x_hi * 2 + x_lo + 3) % 4) // 2
    info = jnp.stack([z, x_hi, core, row, row + 1 - 2 * core, half_owned, y, 1 + 2 * core])
    order = Order(info, unit_slots(cutoffs, core, UNITS), cutoffs)
    most = jnp.maximum(jnp.sum(kept_units(cutoffs, 0)), jnp.sum(kept_units(cutoffs, 1)))
    wait, ready = order.wait, order.ready
    fwd_table, inv_table = long_tables()
    fwd_turned = jnp.asarray(fwd_table.transpose(0, 2, 1))
    inv_turned = jnp.asarray(inv_table.transpose(0, 2, 1))
    fwd_table, inv_table = jnp.asarray(fwd_table), jnp.asarray(inv_table)
    lat_np = latitude_table()
    lat_table = jnp.asarray(lat_np)
    lat_turned = jnp.asarray(lat_np.transpose(0, 2, 1))

    f_own, f_send = wait(*lon_forward(order.scalars, field_in, fwd_table, gain))
    f_recv = swap(f_send, "f_pair", fc=1)
    g_own, g_send = wait(*lon_forward(order.scalars, grad_out, inv_table))
    f_recv = wait(f_recv)
    g_recv = swap(*ready(g_send), "g_pair", fc=1)

    f0a, f0b, f1a, f1b, f2a, f2b, f3a, f3b, f_over = wait(
        *lat_forward(order.scalars, f_own, f_recv, lat_table, owned)
    )
    fa, fb = onward(f3a, "f3a"), onward(f3b, "f3b")
    g_recv = wait(g_recv)
    g0a, g0b, g1a, g1b, g2a, g2b, g3a, g3b, g_over = wait(
        *lat_forward(order.scalars, g_own, g_recv, lat_table, owned)
    )
    fa = onward(wait(add(f2a, wait(fa))), "f2a")
    fb = onward(wait(add(f2b, wait(fb))), "f2b")
    wide = wait(wide_weights(order.scalars, weights))
    fa = onward(wait(add(f1a, wait(fa))), "f1a")
    fb = onward(wait(add(f1b, wait(fb))), "f1b")
    left = shift(wait(add(f0a, wait(fa))), 1, "f_left")
    (ga,) = ready(g3a)
    ga = onward(ga, "g3a")
    right = shift(wait(add(f0b, wait(fb))), -1, "f_right")
    (gb,) = ready(g3b)
    gb = onward(gb, "g3b")
    ga = onward(wait(add(g2a, wait(ga))), "g2a")
    left = wait(left)
    right = wait(right)
    gb = onward(wait(add(g2b, wait(gb))), "g2b")

    shrunk, given, hidden, slope = wait(
        *spectral_forward(order.scalars, (left, right), wide, biases)
    )
    f0a, f0b = shift(shrunk, -1, "f_back_a"), shift(shrunk, 1, "f_back_b")
    ga = onward(wait(add(g1a, wait(ga))), "g1a")
    gb = onward(wait(add(g1b, wait(gb))), "g1b")
    f0a = wait(f0a)
    f3a = onward(f0a, "f_from3a")
    f0b = wait(f0b)
    f3b = onward(f0b, "f_from3b")
    left = shift(wait(add(g0a, wait(ga))), 1, "g_left")
    right = shift(wait(add(g0b, wait(gb))), -1, "g_right")
    start = ready(f_over, g_over, jnp.zeros((2, SHARE, GC), f32))
    _, f_over, g_over, more = lax.while_loop(
        lambda held: held[0] > 8 * owned,
        lambda held: (
            jnp.zeros((), jnp.int32),
            *past_slots(order, owned, held[1], held[2], wide, biases),
        ),
        (most, *start),
    )
    f_over, g_over, more = wait(f_over, g_over, more)
    f3a = wait(f3a)
    f2a = onward(f3a, "f_from2a")
    left = wait(left)
    right = wait(right)
    f3b = wait(f3b)
    f2b = onward(f3b, "f_from2b")

    bottom, upper, lower, sums = wait(
        *spectral_backward(order.scalars, (left, right), wide, given, slope)
    )
    g0a, g0b = shift(bottom, -1, "g_back_a"), shift(bottom, 1, "g_back_b")
    f2a = wait(f2a)
    f1a = onward(f2a, "f_from1a")
    f2b = wait(f2b)
    f1b = onward(f2b, "f_from1b")
    send, keep = wait(*weight_sums(order.scalars, given, lower, hidden, upper, sums, more))
    f1a = wait(f1a)
    g0a = wait(g0a)
    g3a = onward(g0a, "g_from3a")
    g0b = wait(g0b)
    g3b = onward(g0b, "g_from3b")
    f1b = wait(f1b)

    arrived = swap(*ready(send), "sum_core", fc=1)
    f_own, f_send = wait(
        *lat_inverse(
            order.scalars, (f0a, f0b, f1a, f1b, f2a, f2b, f3a, f3b), f_over, lat_turned, owned
        )
    )
    f_recv = swap(f_send, "f_pair_back", fc=1)
    g3a = wait(g3a)
    g2a = onward(g3a, "g_from2a")
    g3b = wait(g3b)
    g2b = onward(g3b, "g_from2b")
    arrived = wait(arrived)
    pieces = wait(*split_sum(order.scalars, keep, arrived))
    arrived = [
        swap(piece, "sum_y", fy=far) for far, piece in zip((1, 2, 3), ready(*pieces[1:]))
    ]
    g2a = wait(g2a)
    g1a = onward(g2a, "g_from1a")
    g2b = wait(g2b)
    g1b = onward(g2b, "g_from1b")
    arrived = wait(*arrived)
    total = wait(four(pieces[0], *arrived))
    beside = swap(total, "sum_x1", fx=1)
    g1a = wait(g1a)
    total = wait(add(total, wait(beside)))
    beside = swap(total, "sum_x2", fx=2)
    g1b = wait(g1b)
    total = wait(add(total, wait(beside)))
    beside = swap(total, "sum_z1", fz=1)
    g_own, g_send = wait(
        *lat_inverse(
            order.scalars, (g0a, g0b, g1a, g1b, g2a, g2b, g3a, g3b), g_over, lat_turned, owned
        )
    )
    g_recv = swap(g_send, "g_pair_back", fc=1)
    total = wait(add(total, wait(beside)))
    beside = swap(total, "sum_z2", fz=2)
    f_recv = wait(f_recv)
    block_out = wait(
        lon_inverse_fields(order.scalars, f_own, f_recv, inv_turned, field_in)
    )
    total = wait(add(total, wait(beside)))
    total = wait(jnp.stack([total, wait(swap(total, "all_core", fc=1))]))
    arrived = [swap(total, "all_y", fy=far) for far in (1, 2, 3)]
    g_recv = wait(g_recv)
    input_grad = wait(
        lon_inverse_grad(order.scalars, g_own, g_recv, fwd_turned, field_in, grad_out, gain)
    )
    arrived = wait(*arrived)
    weight_grads, bias_grads, gain_grad = place_sums(
        order.scalars, (total, *arrived), gain
    )
    return (block_out[None], input_grad[None], weight_grads, bias_grads, gain_grad)


def body(fields, cotangent, norm_gain, weights, biases, cutoffs):
    operands = (fields[0], cotangent[0], norm_gain, weights, biases, cutoffs)
    return whole_pass(OWNED, *operands)


OWNED = 16


def solution(mesh):
    placed = (P("dp", "row", None, None), P("dp", "row", None, None), P(), P(), P(), P())
    return jax.shard_map(
        body,
        mesh=mesh,
        in_specs=placed,
        out_specs=(P("dp", "row", None, None), P("dp", "row", None, None), P(), P(), P()),
        check_vma=False,
    )
```

profile of v0, /device:TPU:6, one launch (start us, length us, event | category | flops | bytes accessed | tf_op | source)
XLA Modules:
  0.0 191.3 jit_solution(10146471326291243852)
XLA Ops:
  1.9 7.7 %lon_forward.2 = (bf16[8,11,16,768]{3,2,1,0:T(8,128)(2,1)}, bf16[8,11,16,768]{3,2,1,0:T(8,128)(2,1)}) custom-call(s32[8]{0:T(128)S(1)} %stack.58.info, s32[176]{0:T(256)S(1)} %convert_reduce_fusion.slots, s32[16]{0:T(128)} %cuts.27, bf16[2,176,360]{2,1,0:T(8,128)(2,1)} %constant.127.clone.own_t.beside_t, ...), custom_call_target="tpu_custom_call" | custom-call | tf_op jit(solution)/shard_map/lon_forward/pallas_call | solution.py:182
  9.6 6.1 %lon_forward.3 = (bf16[8,11,16,768]{3,2,1,0:T(8,128)(2,1)}, bf16[8,11,16,768]{3,2,1,0:T(8,128)(2,1)}) custom-call(s32[8]{0:T(128)S(1)} %stack.58.info, s32[176]{0:T(256)S(1)} %convert_reduce_fusion.slots, s32[16]{0:T(128)S(1)} %copy-done.12, bf16[2,176,360]{2,1,0:T(8,128)(2,1)} %constant.128.clone.own_t.beside_t, ...), custom_call_target="tpu_custom_call" | custom-call | tf_op jit(solution)/shard_map/lon_forward/pallas_call | solution.py:182
  16.2 6.7 %lat_forward.2 = (bf16[16,16,768]{2,1,0:T(8,128)(2,1)}, bf16[16,16,768]{2,1,0:T(8,128)(2,1)}, bf16[16,16,768]{2,1,0:T(8,128)(2,1)}, bf16[16,16,768]{2,1,0:T(8,12...) custom-call(s32[8]{0:T(128)S(1)} %stack.58.info, ...), custom_call_target="tpu_custom_call" | custom-call | tf_op jit(solution)/shard_map/lat_forward/pallas_call | solution.py:236
  23.0 2.0 %collective-permute-start.3 = (bf16[16,16,768]{2,1,0:T(8,128)(2,1)}, bf16[16,16,768]{2,1,0:T(8,128)(2,1)S(1)}, u32[]{:S(2)}, u32[]{:S(2)}) collective-permute-start(bf16[16,16,768]{2,1,0:T(8,128)(2,1)} %get-tuple-element.344), channel_id=1, source_target_pairs={{0,4},{1,13},{2,6},{3,15},{4,8},{5,1},{6,10},{7,3},{8,12},{9,5},{1... | collective-permute-start | bytes 1179656 | tf_op jit(solution)/shard_map/f3a/ppermute | solution.py:96
  24.9 1.9 %collective-permute-start.2 = (bf16[16,16,768]{2,1,0:T(8,128)(2,1)}, bf16[16,16,768]{2,1,0:T(8,128)(2,1)S(1)}, u32[]{:S(2)}, u32[]{:S(2)}) collective-permute-start(bf16[16,16,768]{2,1,0:T(8,128)(2,1)} %get-tuple-element.342), channel_id=1, source_target_pairs={{0,4},{1,13},{2,6},{3,15},{4,8},{5,1},{6,10},{7,3},{8,12},{9,5},{1... | collective-permute-start | bytes 1179656 | tf_op jit(solution)/shard_map/f3b/ppermute | solution.py:96
  26.9 6.8 %lat_forward.3 = (bf16[16,16,768]{2,1,0:T(8,128)(2,1)}, bf16[16,16,768]{2,1,0:T(8,128)(2,1)}, bf16[16,16,768]{2,1,0:T(8,128)(2,1)}, bf16[16,16,768]{2,1,0:T(8,12...) custom-call(s32[8]{0:T(128)S(1)} %stack.58.info, ...), custom_call_target="tpu_custom_call" | custom-call | tf_op jit(solution)/shard_map/lat_forward/pallas_call | solution.py:236
  33.8 1.7 collective-permute-start.5
  35.5 1.8 collective-permute-done.2
  37.5 1.8 wide_weights.1.rest_1_.rest_2_
  39.3 3.6 %collective-permute-done.5 = bf16[16,16,768]{2,1,0:T(8,128)(2,1)S(1)} collective-permute-done((bf16[16,16,768]{2,1,0:T(8,128)(2,1)S(1)}, bf16[16,16,768]{2,1,0:T(8,128)(2,1)S(1)}, u32[]{:S(2)}, u32[]{:S(2)}) %collective-permute-start.5) | collective-permute-done | bytes 393248 | tf_op jit(solution)/shard_map/f2a/ppermute | solution.py:96
  43.5 3.6 %collective-permute-done.4 = bf16[16,16,768]{2,1,0:T(8,128)(2,1)S(1)} collective-permute-done((bf16[16,16,768]{2,1,0:T(8,128)(2,1)S(1)}, bf16[16,16,768]{2,1,0:T(8,128)(2,1)S(1)}, u32[]{:S(2)}, u32[]{:S(2)}) %collective-permute-start.4) | collective-permute-done | bytes 393248 | tf_op jit(solution)/shard_map/f2b/ppermute | solution.py:96
  47.7 4.4 %collective-permute-done.7 = bf16[16,16,768]{2,1,0:T(8,128)(2,1)S(1)} collective-permute-done((bf16[16,16,768]{2,1,0:T(8,128)(2,1)S(1)}, bf16[16,16,768]{2,1,0:T(8,128)(2,1)S(1)}, u32[]{:S(2)}, u32[]{:S(2)}) %collective-permute-start.7) | collective-permute-done | bytes 393248 | tf_op jit(solution)/shard_map/f1a/ppermute | solution.py:96
  52.2 4.0 %collective-permute-done.6 = bf16[16,16,768]{2,1,0:T(8,128)(2,1)S(1)} collective-permute-done((bf16[16,16,768]{2,1,0:T(8,128)(2,1)S(1)}, bf16[16,16,768]{2,1,0:T(8,128)(2,1)S(1)}, u32[]{:S(2)}, u32[]{:S(2)}) %collective-permute-start.6) | collective-permute-done | bytes 393248 | tf_op jit(solution)/shard_map/f1b/ppermute | solution.py:96
  58.5 2.7 %collective-permute-done.11 = bf16[16,16,768]{2,1,0:T(8,128)(2,1)S(1)} collective-permute-done((bf16[16,16,768]{2,1,0:T(8,128)(2,1)S(1)}, bf16[16,16,768]{2,1,0:T(8,128)(2,1)S(1)}, u32[]{:S(2)}, u32[]{:S(2)}) %collective-permute-start.11) | collective-permute-done | bytes 393248 | tf_op jit(solution)/shard_map/g3a/ppermute | solution.py:96
  61.3 3.2 %collective-permute-done.10.xl = bf16[16,16,768]{2,1,0:T(8,128)(2,1)S(1)} collective-permute-done((bf16[16,16,768]{2,1,0:T(8,128)(2,1)S(1)}, bf16[16,16,768]{2,1,0:T(8,128)(2,1)S(1)}, u32[]{:S(2)}, u32[]{:S(2)}) %collective-permute-start.10) | collective-permute-done | bytes 393248 | tf_op jit(solution)/shard_map/f_left/ppermute | solution.py:87
  66.1 1.6 collective-permute-start.15
  68.1 2.4 %spectral_forward.3 = (bf16[16,16,768]{2,1,0:T(8,128)(2,1)S(1)}, bf16[2,128,768]{2,1,0:T(8,128)(2,1)S(1)}, bf16[2,128,768]{2,1,0:T(8,128)(2,1)S(1)}, f32[2,128,768]{2,1,0:T(8,128)S(1)}) custom-call(s32[8]{0:T(128)S(1)} %stack.58.info, s32[176]{0:T(256)S(1)} %convert_reduce_fusion.slots, s32[16]{0:T(128)S(1)} %copy-done.12, ...), custom_call_target="tpu_custom_call" | custom-call | tf_op jit(solution)/shard_map/spectral_forward/pallas_call | solution.py:453
  71.9 2.7 %collective-permute-start.12 = (bf16[16,16,768]{2,1,0:T(8,128)(2,1)S(1)}, bf16[16,16,768]{2,1,0:T(8,128)(2,1)}, u32[]{:S(2)}, u32[]{:S(2)}) collective-permute-start(bf16[16,16,768]{2,1,0:T(8,128)(2,1)S(1)} %get-tuple-element.392), channel_id=1, source_target_pairs={{0,16},{1,17},{2,18},{3,19},{4,20},{5,21},{6,22},{7,23},{8,24},{9,... | collective-permute-start | bytes 1179656 | tf_op jit(solution)/shard_map/f_back_b/ppermute | solution.py:87
  75.2 2.1 %collective-permute-start.18 = (bf16[16,16,768]{2,1,0:T(8,128)(2,1)S(1)}, bf16[16,16,768]{2,1,0:T(8,128)(2,1)S(1)}, u32[]{:S(2)}, u32[]{:S(2)}) collective-permute-start(bf16[16,16,768]{2,1,0:T(8,128)(2,1)S(1)} %add_convert_fusion.3), channel_id=1, source_target_pairs={{0,4},{1,13},{2,6},{3,15},{4,8},{5,1},{6,10},{7,3},{8,12},{9,5},{1... | collective-permute-start | bytes 1179656 | tf_op jit(solution)/shard_map/g1a/ppermute | solution.py:96
  77.3 2.0 %collective-permute-done.14 = bf16[16,16,768]{2,1,0:T(8,128)(2,1)S(1)} collective-permute-done((bf16[16,16,768]{2,1,0:T(8,128)(2,1)S(1)}, bf16[16,16,768]{2,1,0:T(8,128)(2,1)S(1)}, u32[]{:S(2)}, u32[]{:S(2)}) %collective-permute-start.14) | collective-permute-done | bytes 393248 | tf_op jit(solution)/shard_map/g2b/ppermute | solution.py:96
  83.5 1.7 collective-permute-start.21
  86.1 2.5 %collective-permute-done.17 = bf16[16,16,768]{2,1,0:T(8,128)(2,1)} collective-permute-done((bf16[16,16,768]{2,1,0:T(8,128)(2,1)S(1)}, bf16[16,16,768]{2,1,0:T(8,128)(2,1)}, u32[]{:S(2)}, u32[]{:S(2)}) %collective-permute-start.17) | collective-permute-done | bytes 393248 | tf_op jit(solution)/shard_map/g1b/ppermute | solution.py:96
  88.6 1.9 add_convert_fusion
  94.5 4.1 %collective-permute-done.20.xl = bf16[16,16,768]{2,1,0:T(8,128)(2,1)} collective-permute-done((bf16[16,16,768]{2,1,0:T(8,128)(2,1)}, bf16[16,16,768]{2,1,0:T(8,128)(2,1)}, u32[]{:S(2)}, u32[]{:S(2)}) %collective-permute-start.20) | collective-permute-done | bytes 393248 | tf_op jit(solution)/shard_map/g_left/ppermute | solution.py:87
  98.5 1.6 collective-permute-done.19.rest_0_
  101.7 4.4 %spectral_backward.3 = (bf16[16,16,768]{2,1,0:T(8,128)(2,1)S(1)}, bf16[2,128,768]{2,1,0:T(8,128)(2,1)S(1)}, bf16[2,128,768]{2,1,0:T(8,128)(2,1)S(1)}, f32[2,8,768]{2,1,0:T(8,128)S(1)}) custom-call(s32[8]{0:T(128)S(1)} %get-tuple-element.649, s32[176]{0:T(256)S(1)} %get-tuple-element.650, s32[16]{0:T(128)S(1)} %get-tuple-element.651, ...), custom_call_target="tpu_custom_call" | custom-call | tf_op jit(solution)/shard_map/spectral_backward/pallas_call | solution.py:486
  106.2 1.8 collective-permute-start.27
  108.0 3.2 %collective-permute-start.25 = (bf16[16,16,768]{2,1,0:T(8,128)(2,1)S(1)}, bf16[16,16,768]{2,1,0:T(8,128)(2,1)S(1)}, u32[]{:S(2)}, u32[]{:S(2)}) collective-permute-start(bf16[16,16,768]{2,1,0:T(8,128)(2,1)S(1)} %get-tuple-element.446), channel_id=1, source_target_pairs={{0,16},{1,17},{2,18},{3,19},{4,20},{5,21},{6,22},{7,23},{8,24},{9,... | collective-permute-start | bytes 1179656 | tf_op jit(solution)/shard_map/g_back_b/ppermute | solution.py:87
  112.6 2.3 %weight_sums.3 = (bf16[416,384]{1,0:T(8,128)(2,1)S(1)}, f32[416,384]{1,0:T(8,128)S(1)}) custom-call(s32[8]{0:T(128)S(1)} %get-tuple-element.649, s32[176]{0:T(256)S(1)} %get-tuple-element.650, s32[16]{0:T(128)S(1)} %get-tuple-element.651, bf16[2,128,768]{2,1,0:T(8,128)(2,1)S(1)} %get-tuple-element.437.rest_3_.u0, ...), custom_call_target="tpu_custom_call" | custom-call | tf_op jit(solution)/shard_map/weight_sums/pallas_call | solution.py:542
  115.2 1.7 collective-permute-done.26.rest_0_
  118.4 1.8 collective-permute-done.24.rest_3_
  120.2 5.9 %lat_inverse.2 = (bf16[8,11,16,768]{3,2,1,0:T(8,128)(2,1)}, bf16[8,11,16,768]{3,2,1,0:T(8,128)(2,1)}) custom-call(s32[8]{0:T(128)S(1)} %get-tuple-element.649, s32[176]{0:T(256)S(1)} %get-tuple-element.650, s32[16]{0:T(128)S(1)} %get-tuple-element.651, bf16[16,128,256]{2,1,0:T(8,128)(2,1)S(1)} %copy-done.1, bf16[16,128,256]{2,1,0:T(8,128)(2,1)S(1)} %copy-done.1, ...), custom_call_target="tpu_custom_call" | custom-call | tf_op jit(solution)/shard_map/lat_inverse/pallas_call | solution.py:273
  126.4 3.8 %collective-permute-done.30.rest_7_ = bf16[16,16,768]{2,1,0:T(8,128)(2,1)S(1)} collective-permute-done((bf16[16,16,768]{2,1,0:T(8,128)(2,1)S(1)}, bf16[16,16,768]{2,1,0:T(8,128)(2,1)S(1)}, u32[]{:S(2)}, u32[]{:S(2)}) %collective-permute-start.30) | collective-permute-done | bytes 393248 | tf_op jit(solution)/shard_map/g_from3b/ppermute | solution.py:96
  131.0 1.7 collective-permute-start.32
  132.6 2.9 %collective-permute-start.33 = (bf16[104,384]{1,0:T(8,128)(2,1)S(1)}, bf16[104,384]{1,0:T(8,128)(2,1)S(1)}, u32[]{:S(2)}, u32[]{:S(2)}) collective-permute-start(bf16[104,384]{1,0:T(8,128)(2,1)S(1)} %get-tuple-element.487), channel_id=1, source_target_pairs={{0,64},{1,65},{2,66},{3,67},{4,68},{5,69},{6,70},{7,71},{8,72},{9,... | collective-permute-start | bytes 239624 | tf_op jit(solution)/shard_map/sum_y/ppermute | solution.py:105
  135.8 3.6 %collective-permute-done.35.rest_5_ = bf16[16,16,768]{2,1,0:T(8,128)(2,1)S(1)} collective-permute-done((bf16[16,16,768]{2,1,0:T(8,128)(2,1)S(1)}, bf16[16,16,768]{2,1,0:T(8,128)(2,1)S(1)}, u32[]{:S(2)}, u32[]{:S(2)}) %collective-permute-start.35) | collective-permute-done | bytes 393248 | tf_op jit(solution)/shard_map/g_from2b/ppermute | solution.py:96
  139.4 1.7 collective-permute-done.34
  141.4 3.3 %collective-permute-done.38.rest_2_ = bf16[16,16,768]{2,1,0:T(8,128)(2,1)S(1)} collective-permute-done((bf16[16,16,768]{2,1,0:T(8,128)(2,1)S(1)}, bf16[16,16,768]{2,1,0:T(8,128)(2,1)S(1)}, u32[]{:S(2)}, u32[]{:S(2)}) %collective-permute-start.38) | collective-permute-done | bytes 393248 | tf_op jit(solution)/shard_map/g_from1a/ppermute | solution.py:96
  146.1 2.9 %collective-permute-done.40.rest_3_ = bf16[16,16,768]{2,1,0:T(8,128)(2,1)S(1)} collective-permute-done((bf16[16,16,768]{2,1,0:T(8,128)(2,1)S(1)}, bf16[16,16,768]{2,1,0:T(8,128)(2,1)S(1)}, u32[]{:S(2)}, u32[]{:S(2)}) %collective-permute-start.40) | collective-permute-done | bytes 393248 | tf_op jit(solution)/shard_map/g_from1b/ppermute | solution.py:96
  148.9 2.8 %collective-permute-done.39 = bf16[104,384]{1,0:T(8,128)(2,1)S(1)} collective-permute-done((bf16[104,384]{1,0:T(8,128)(2,1)S(1)}, bf16[104,384]{1,0:T(8,128)(2,1)S(1)}, u32[]{:S(2)}, u32[]{:S(2)}) %collective-permute-start.39) | collective-permute-done | bytes 79904 | tf_op jit(solution)/shard_map/sum_x2/ppermute | solution.py:105
  151.8 4.8 %lat_inverse.3 = (bf16[8,11,16,768]{3,2,1,0:T(8,128)(2,1)}, bf16[8,11,16,768]{3,2,1,0:T(8,128)(2,1)}) custom-call(s32[8]{0:T(128)S(1)} %get-tuple-element.649, s32[176]{0:T(256)S(1)} %get-tuple-element.650, s32[16]{0:T(128)S(1)} %get-tuple-element.651, bf16[16,128,256]{2,1,0:T(8,128)(2,1)S(1)} %copy-done.1, bf16[16,128,256]{2,1,0:T(8,128)(2,1)S(1)} %copy-done.1, ...), custom_call_target="tpu_custom_call" | custom-call | tf_op jit(solution)/shard_map/lat_inverse/pallas_call | solution.py:273
  156.7 4.7 %collective-permute-done.41 = bf16[104,384]{1,0:T(8,128)(2,1)S(1)} collective-permute-done((bf16[104,384]{1,0:T(8,128)(2,1)S(1)}, bf16[104,384]{1,0:T(8,128)(2,1)S(1)}, u32[]{:S(2)}, u32[]{:S(2)}) %collective-permute-start.41) | collective-permute-done | bytes 79904 | tf_op jit(solution)/shard_map/sum_z1/ppermute | solution.py:105
  161.4 3.7 %collective-permute-start.43 = (bf16[104,384]{1,0:T(8,128)(2,1)S(1)}, bf16[104,384]{1,0:T(8,128)(2,1)S(1)}, u32[]{:S(2)}, u32[]{:S(2)}) collective-permute-start(bf16[104,384]{1,0:T(8,128)(2,1)S(1)} %add_convert_fusion.13), channel_id=1, source_target_pairs={{0,8},{1,9},{2,10},{3,11},{4,12},{5,13},{6,14},{7,15},{8,0},{9,1},... | collective-permute-start | bytes 239624 | tf_op jit(solution)/shard_map/sum_z2/ppermute | solution.py:105
  165.1 6.8 %lon_inverse_fields.1 = bf16[8,360,768]{2,1,0:T(8,128)(2,1)} custom-call(s32[8]{0:T(128)S(1)} %get-tuple-element.649, s32[176]{0:T(256)S(1)} %get-tuple-element.650, s32[16]{0:T(128)S(1)} %get-tuple-element.651, bf16[2,360,176]{2,1,0:T(8,128)(2,1)S(1)} %copy-done.3, bf16[2,360,176]{2,1,0:T(8,128)(2,1)S(1)} %copy-done.3, ...), custom_call_target="tpu_custom_call" | custom-call | tf_op jit(solution)/shard_map/lon_inverse_fields/pallas_call | solution.py:300
  173.4 2.7 %collective-permute-start.46 = (bf16[2,104,384]{2,1,0:T(8,128)(2,1)S(1)}, bf16[2,104,384]{2,1,0:T(8,128)(2,1)S(1)}, u32[]{:S(2)}, u32[]{:S(2)}) collective-permute-start(bf16[2,104,384]{2,1,0:T(8,128)(2,1)S(1)} %pad_maximum_fusion.p0), channel_id=1, source_target_pairs={{0,64},{1,65},{2,66},{3,67},{4,68},{5,69},{6,70},{7,71},{8,72},{9,... | collective-permute-start | bytes 479240 | tf_op jit(solution)/shard_map/all_y/ppermute | solution.py:105
  176.2 1.9 collective-permute-start.47
  178.1 10.8 %lon_inverse_grad.1 = bf16[8,360,768]{2,1,0:T(8,128)(2,1)} custom-call(s32[8]{0:T(128)S(1)} %get-tuple-element.649, s32[176]{0:T(256)S(1)} %get-tuple-element.650, s32[16]{0:T(128)S(1)} %get-tuple-element.651, bf16[2,360,176]{2,1,0:T(8,128)(2,1)} %constant.125.clone.own_t.beside_t, bf16[2,360,176]{2,1,0:T(8,128)(2,1)} %constant.125.clone.own_t.beside_t, ...), custom_call_target="tpu_custom_call" | custom-call | tf_op jit(solution)/shard_map/lon_inverse_grad/pallas_call | solution.py:327
  188.9 2.4 %place_sums.1 = (f32[2,2,8,96,96]{4,3,2,1,0:T(8,128)}, f32[2,2,768]{2,1,0:T(2,128)}, f32[768]{0:T(1024)}) custom-call(s32[8]{0:T(128)S(1)} %get-tuple-element.649, s32[176]{0:T(256)S(1)} %get-tuple-element.650, s32[16]{0:T(128)S(1)} %get-tuple-element.651, bf16[2,104,384]{2,1,0:T(8,128)(2,1)S(1)} %pad_maximum_fusion.p0, ...), custom_call_target="tpu_custom_call" | custom-call | tf_op jit(solution)/shard_map/place_sums/pallas_call | solution.py:600
  (145 shorter events, 26.6 us)
Async XLA Ops:
  9.6 6.1 %collective-permute-start = (bf16[8,11,16,768]{3,2,1,0:T(8,128)(2,1)}, bf16[8,11,16,768]{3,2,1,0:T(8,128)(2,1)}, u32[]{:S(2)}, u32[]{:S(2)}) collective-permute-start(bf16[8,11,16,768]{3,2,1,0:T(8,128)(2,1)} %get-tuple-element.309), channel_id=1, source_target_pairs={{0,1},{1,0},{2,3},{3,2},{4,5},{5,4},{6,7},{7,6},{8,9},{9,8},{10,11... | collective-permute-start | bytes 6488072 | tf_op jit(solution)/shard_map/f_pair/ppermute | solution.py:105
  15.7 11.2 %collective-permute-start.1 = (bf16[8,11,16,768]{3,2,1,0:T(8,128)(2,1)}, bf16[8,11,16,768]{3,2,1,0:T(8,128)(2,1)}, u32[]{:S(2)}, u32[]{:S(2)}) collective-permute-start(bf16[8,11,16,768]{3,2,1,0:T(8,128)(2,1)} %get-tuple-element.312), channel_id=1, source_target_pairs={{0,1},{1,0},{2,3},{3,2},{4,5},{5,4},{6,7},{7,6},{8,9},{9,8},{10,11... | collective-permute-start | bytes 6488072 | tf_op jit(solution)/shard_map/g_pair/ppermute | solution.py:105
  23.0 10.7 %collective-permute-start.3 = (bf16[16,16,768]{2,1,0:T(8,128)(2,1)}, bf16[16,16,768]{2,1,0:T(8,128)(2,1)S(1)}, u32[]{:S(2)}, u32[]{:S(2)}) collective-permute-start(bf16[16,16,768]{2,1,0:T(8,128)(2,1)} %get-tuple-element.344), channel_id=1, source_target_pairs={{0,4},{1,13},{2,6},{3,15},{4,8},{5,1},{6,10},{7,3},{8,12},{9,5},{1... | collective-permute-start | bytes 1179656 | tf_op jit(solution)/shard_map/f3a/ppermute | solution.py:96
  24.9 12.3 %collective-permute-start.2 = (bf16[16,16,768]{2,1,0:T(8,128)(2,1)}, bf16[16,16,768]{2,1,0:T(8,128)(2,1)S(1)}, u32[]{:S(2)}, u32[]{:S(2)}) collective-permute-start(bf16[16,16,768]{2,1,0:T(8,128)(2,1)} %get-tuple-element.342), channel_id=1, source_target_pairs={{0,4},{1,13},{2,6},{3,15},{4,8},{5,1},{6,10},{7,3},{8,12},{9,5},{1... | collective-permute-start | bytes 1179656 | tf_op jit(solution)/shard_map/f3b/ppermute | solution.py:96
  33.8 9.1 %collective-permute-start.5 = (bf16[16,16,768]{2,1,0:T(8,128)(2,1)S(1)}, bf16[16,16,768]{2,1,0:T(8,128)(2,1)S(1)}, u32[]{:S(2)}, u32[]{:S(2)}) collective-permute-start(bf16[16,16,768]{2,1,0:T(8,128)(2,1)S(1)} %add_convert_fusion.11), channel_id=1, source_target_pairs={{0,4},{1,13},{2,6},{3,15},{4,8},{5,1},{6,10},{7,3},{8,12},{9,5},{1... | collective-permute-start | bytes 1179656 | tf_op jit(solution)/shard_map/f2a/ppermute | solution.py:96
  37.4 9.7 %collective-permute-start.4 = (bf16[16,16,768]{2,1,0:T(8,128)(2,1)S(1)}, bf16[16,16,768]{2,1,0:T(8,128)(2,1)S(1)}, u32[]{:S(2)}, u32[]{:S(2)}) collective-permute-start(bf16[16,16,768]{2,1,0:T(8,128)(2,1)S(1)} %add_convert_fusion.10), channel_id=1, source_target_pairs={{0,4},{1,13},{2,6},{3,15},{4,8},{5,1},{6,10},{7,3},{8,12},{9,5},{1... | collective-permute-start | bytes 1179656 | tf_op jit(solution)/shard_map/f2b/ppermute | solution.py:96
  43.0 9.1 %collective-permute-start.7 = (bf16[16,16,768]{2,1,0:T(8,128)(2,1)S(1)}, bf16[16,16,768]{2,1,0:T(8,128)(2,1)S(1)}, u32[]{:S(2)}, u32[]{:S(2)}) collective-permute-start(bf16[16,16,768]{2,1,0:T(8,128)(2,1)S(1)} %add_convert_fusion.9), channel_id=1, source_target_pairs={{0,4},{1,13},{2,6},{3,15},{4,8},{5,1},{6,10},{7,3},{8,12},{9,5},{1... | collective-permute-start | bytes 1179656 | tf_op jit(solution)/shard_map/f1a/ppermute | solution.py:96
  47.2 9.1 %collective-permute-start.6 = (bf16[16,16,768]{2,1,0:T(8,128)(2,1)S(1)}, bf16[16,16,768]{2,1,0:T(8,128)(2,1)S(1)}, u32[]{:S(2)}, u32[]{:S(2)}) collective-permute-start(bf16[16,16,768]{2,1,0:T(8,128)(2,1)S(1)} %add_convert_fusion.8), channel_id=1, source_target_pairs={{0,4},{1,13},{2,6},{3,15},{4,8},{5,1},{6,10},{7,3},{8,12},{9,5},{1... | collective-permute-start | bytes 1179656 | tf_op jit(solution)/shard_map/f1b/ppermute | solution.py:96
  52.2 9.1 %collective-permute-start.11 = (bf16[16,16,768]{2,1,0:T(8,128)(2,1)S(1)}, bf16[16,16,768]{2,1,0:T(8,128)(2,1)S(1)}, u32[]{:S(2)}, u32[]{:S(2)}) collective-permute-start(bf16[16,16,768]{2,1,0:T(8,128)(2,1)S(1)} %copy-done.27), channel_id=1, source_target_pairs={{0,4},{1,13},{2,6},{3,15},{4,8},{5,1},{6,10},{7,3},{8,12},{9,5},{1... | collective-permute-start | bytes 1179656 | tf_op jit(solution)/shard_map/g3a/ppermute | solution.py:96
  56.2 8.3 %collective-permute-start.10 = (bf16[16,16,768]{2,1,0:T(8,128)(2,1)S(1)}, bf16[16,16,768]{2,1,0:T(8,128)(2,1)S(1)}, u32[]{:S(2)}, u32[]{:S(2)}) collective-permute-start(bf16[16,16,768]{2,1,0:T(8,128)(2,1)S(1)} %add_convert_fusion.7), channel_id=1, source_target_pairs={{0,16},{1,17},{2,18},{3,19},{4,20},{5,21},{6,22},{7,23},{8,24},{9,... | collective-permute-start | bytes 1179656 | tf_op jit(solution)/shard_map/f_left/ppermute | solution.py:87
  56.8 9.3 %collective-permute-start.9 = (bf16[16,16,768]{2,1,0:T(8,128)(2,1)S(1)}, bf16[16,16,768]{2,1,0:T(8,128)(2,1)S(1)}, u32[]{:S(2)}, u32[]{:S(2)}) collective-permute-start(bf16[16,16,768]{2,1,0:T(8,128)(2,1)S(1)} %add_convert_fusion.6), channel_id=1, source_target_pairs={{0,18},{1,19},{2,16},{3,17},{4,22},{5,23},{6,20},{7,21},{8,26},{9,... | collective-permute-start | bytes 1179656 | tf_op jit(solution)/shard_map/f_right/ppermute | solution.py:87
  58.5 9.3 %collective-permute-start.8 = (bf16[16,16,768]{2,1,0:T(8,128)(2,1)S(1)}, bf16[16,16,768]{2,1,0:T(8,128)(2,1)S(1)}, u32[]{:S(2)}, u32[]{:S(2)}) collective-permute-start(bf16[16,16,768]{2,1,0:T(8,128)(2,1)S(1)} %copy-done.26), channel_id=1, source_target_pairs={{0,4},{1,13},{2,6},{3,15},{4,8},{5,1},{6,10},{7,3},{8,12},{9,5},{1... | collective-permute-start | bytes 1179656 | tf_op jit(solution)/shard_map/g3b/ppermute | solution.py:96
  66.1 9.0 %collective-permute-start.15 = (bf16[16,16,768]{2,1,0:T(8,128)(2,1)S(1)}, bf16[16,16,768]{2,1,0:T(8,128)(2,1)S(1)}, u32[]{:S(2)}, u32[]{:S(2)}) collective-permute-start(bf16[16,16,768]{2,1,0:T(8,128)(2,1)S(1)} %add_convert_fusion.5), channel_id=1, source_target_pairs={{0,4},{1,13},{2,6},{3,15},{4,8},{5,1},{6,10},{7,3},{8,12},{9,5},{1... | collective-permute-start | bytes 1179656 | tf_op jit(solution)/shard_map/g2a/ppermute | solution.py:96
  67.9 11.4 %collective-permute-start.14 = (bf16[16,16,768]{2,1,0:T(8,128)(2,1)S(1)}, bf16[16,16,768]{2,1,0:T(8,128)(2,1)S(1)}, u32[]{:S(2)}, u32[]{:S(2)}) collective-permute-start(bf16[16,16,768]{2,1,0:T(8,128)(2,1)S(1)} %add_convert_fusion.4), channel_id=1, source_target_pairs={{0,4},{1,13},{2,6},{3,15},{4,8},{5,1},{6,10},{7,3},{8,12},{9,5},{1... | collective-permute-start | bytes 1179656 | tf_op jit(solution)/shard_map/g2b/ppermute | solution.py:96
  71.4 12.1 %collective-permute-start.13 = (bf16[16,16,768]{2,1,0:T(8,128)(2,1)S(1)}, bf16[16,16,768]{2,1,0:T(8,128)(2,1)}, u32[]{:S(2)}, u32[]{:S(2)}) collective-permute-start(bf16[16,16,768]{2,1,0:T(8,128)(2,1)S(1)} %get-tuple-element.392), channel_id=1, source_target_pairs={{0,18},{1,19},{2,16},{3,17},{4,22},{5,23},{6,20},{7,21},{8,26},{9,... | collective-permute-start | bytes 1179656 | tf_op jit(solution)/shard_map/f_back_a/ppermute | solution.py:87
  71.9 11.5 %collective-permute-start.12 = (bf16[16,16,768]{2,1,0:T(8,128)(2,1)S(1)}, bf16[16,16,768]{2,1,0:T(8,128)(2,1)}, u32[]{:S(2)}, u32[]{:S(2)}) collective-permute-start(bf16[16,16,768]{2,1,0:T(8,128)(2,1)S(1)} %get-tuple-element.392), channel_id=1, source_target_pairs={{0,16},{1,17},{2,18},{3,19},{4,20},{5,21},{6,22},{7,23},{8,24},{9,... | collective-permute-start | bytes 1179656 | tf_op jit(solution)/shard_map/f_back_b/ppermute | solution.py:87
  75.2 10.0 %collective-permute-start.18 = (bf16[16,16,768]{2,1,0:T(8,128)(2,1)S(1)}, bf16[16,16,768]{2,1,0:T(8,128)(2,1)S(1)}, u32[]{:S(2)}, u32[]{:S(2)}) collective-permute-start(bf16[16,16,768]{2,1,0:T(8,128)(2,1)S(1)} %add_convert_fusion.3), channel_id=1, source_target_pairs={{0,4},{1,13},{2,6},{3,15},{4,8},{5,1},{6,10},{7,3},{8,12},{9,5},{1... | collective-permute-start | bytes 1179656 | tf_op jit(solution)/shard_map/g1a/ppermute | solution.py:96
  79.4 9.2 %collective-permute-start.17 = (bf16[16,16,768]{2,1,0:T(8,128)(2,1)S(1)}, bf16[16,16,768]{2,1,0:T(8,128)(2,1)}, u32[]{:S(2)}, u32[]{:S(2)}) collective-permute-start(bf16[16,16,768]{2,1,0:T(8,128)(2,1)S(1)} %add_convert_fusion.2), channel_id=1, source_target_pairs={{0,4},{1,13},{2,6},{3,15},{4,8},{5,1},{6,10},{7,3},{8,12},{9,5},{1... | collective-permute-start | bytes 1179656 | tf_op jit(solution)/shard_map/g1b/ppermute | solution.py:96
  83.5 10.1 %collective-permute-start.21 = (bf16[16,16,768]{2,1,0:T(8,128)(2,1)}, bf16[16,16,768]{2,1,0:T(8,128)(2,1)}, u32[]{:S(2)}, u32[]{:S(2)}) collective-permute-start(bf16[16,16,768]{2,1,0:T(8,128)(2,1)} %collective-permute-done.13.rest_0_), channel_id=1, source_target_pairs={{0,4},{1,13},{2,6},{3,15},{4,8},{5,1},{6,10},{7,3},{8,12},{9,5},{1... | collective-permute-start | bytes 1179656 | tf_op jit(solution)/shard_map/f_from3a/ppermute | solution.py:96
  85.2 15.0 %collective-permute-start.16 = (bf16[16,16,768]{2,1,0:T(8,128)(2,1)}, bf16[16,16,768]{2,1,0:T(8,128)(2,1)}, u32[]{:S(2)}, u32[]{:S(2)}) collective-permute-start(bf16[16,16,768]{2,1,0:T(8,128)(2,1)} %collective-permute-done.12.rest_1_), channel_id=1, source_target_pairs={{0,4},{1,13},{2,6},{3,15},{4,8},{5,1},{6,10},{7,3},{8,12},{9,5},{1... | collective-permute-start | bytes 1179656 | tf_op jit(solution)/shard_map/f_from3b/ppermute | solution.py:96
  90.4 8.1 %collective-permute-start.20 = (bf16[16,16,768]{2,1,0:T(8,128)(2,1)}, bf16[16,16,768]{2,1,0:T(8,128)(2,1)}, u32[]{:S(2)}, u32[]{:S(2)}) collective-permute-start(bf16[16,16,768]{2,1,0:T(8,128)(2,1)} %add_convert_fusion.1), channel_id=1, source_target_pairs={{0,16},{1,17},{2,18},{3,19},{4,20},{5,21},{6,22},{7,23},{8,24},{9,... | collective-permute-start | bytes 1179656 | tf_op jit(solution)/shard_map/g_left/ppermute | solution.py:87
  90.9 9.3 %collective-permute-start.19 = (bf16[16,16,768]{2,1,0:T(8,128)(2,1)}, bf16[16,16,768]{2,1,0:T(8,128)(2,1)}, u32[]{:S(2)}, u32[]{:S(2)}) collective-permute-start(bf16[16,16,768]{2,1,0:T(8,128)(2,1)} %add_convert_fusion), channel_id=1, source_target_pairs={{0,18},{1,19},{2,16},{3,17},{4,22},{5,23},{6,20},{7,21},{8,26},{9,... | collective-permute-start | bytes 1179656 | tf_op jit(solution)/shard_map/g_right/ppermute | solution.py:87
  93.6 12.6 %collective-permute-start.23 = (bf16[16,16,768]{2,1,0:T(8,128)(2,1)}, bf16[16,16,768]{2,1,0:T(8,128)(2,1)S(1)}, u32[]{:S(2)}, u32[]{:S(2)}) collective-permute-start(bf16[16,16,768]{2,1,0:T(8,128)(2,1)} %collective-permute-done.21.rest_6_), channel_id=1, source_target_pairs={{0,4},{1,13},{2,6},{3,15},{4,8},{5,1},{6,10},{7,3},{8,12},{9,5},{1... | collective-permute-start | bytes 1179656 | tf_op jit(solution)/shard_map/f_from2a/ppermute | solution.py:96
  100.2 11.0 %collective-permute-start.22 = (bf16[16,16,768]{2,1,0:T(8,128)(2,1)}, bf16[16,16,768]{2,1,0:T(8,128)(2,1)S(1)}, u32[]{:S(2)}, u32[]{:S(2)}) collective-permute-start(bf16[16,16,768]{2,1,0:T(8,128)(2,1)} %collective-permute-done.16.rest_7_), channel_id=1, source_target_pairs={{0,4},{1,13},{2,6},{3,15},{4,8},{5,1},{6,10},{7,3},{8,12},{9,5},{1... | collective-permute-start | bytes 1179656 | tf_op jit(solution)/shard_map/f_from2b/ppermute | solution.py:96
  106.2 9.1 %collective-permute-start.27 = (bf16[16,16,768]{2,1,0:T(8,128)(2,1)S(1)}, bf16[16,16,768]{2,1,0:T(8,128)(2,1)S(1)}, u32[]{:S(2)}, u32[]{:S(2)}) collective-permute-start(bf16[16,16,768]{2,1,0:T(8,128)(2,1)S(1)} %collective-permute-done.23.rest_4_), channel_id=1, source_target_pairs={{0,4},{1,13},{2,6},{3,15},{4,8},{5,1},{6,10},{7,3},{8,12},{9,5},{1... | collective-permute-start | bytes 1179656 | tf_op jit(solution)/shard_map/f_from1a/ppermute | solution.py:96
  108.0 9.0 %collective-permute-start.26 = (bf16[16,16,768]{2,1,0:T(8,128)(2,1)S(1)}, bf16[16,16,768]{2,1,0:T(8,128)(2,1)S(1)}, u32[]{:S(2)}, u32[]{:S(2)}) collective-permute-start(bf16[16,16,768]{2,1,0:T(8,128)(2,1)S(1)} %get-tuple-element.446), channel_id=1, source_target_pairs={{0,18},{1,19},{2,16},{3,17},{4,22},{5,23},{6,20},{7,21},{8,26},{9,... | collective-permute-start | bytes 1179656 | tf_op jit(solution)/shard_map/g_back_a/ppermute | solution.py:87
  108.0 10.4 %collective-permute-start.25 = (bf16[16,16,768]{2,1,0:T(8,128)(2,1)S(1)}, bf16[16,16,768]{2,1,0:T(8,128)(2,1)S(1)}, u32[]{:S(2)}, u32[]{:S(2)}) collective-permute-start(bf16[16,16,768]{2,1,0:T(8,128)(2,1)S(1)} %get-tuple-element.446), channel_id=1, source_target_pairs={{0,16},{1,17},{2,18},{3,19},{4,20},{5,21},{6,22},{7,23},{8,24},{9,... | collective-permute-start | bytes 1179656 | tf_op jit(solution)/shard_map/g_back_b/ppermute | solution.py:87
  111.2 9.0 %collective-permute-start.24 = (bf16[16,16,768]{2,1,0:T(8,128)(2,1)S(1)}, bf16[16,16,768]{2,1,0:T(8,128)(2,1)S(1)}, u32[]{:S(2)}, u32[]{:S(2)}) collective-permute-start(bf16[16,16,768]{2,1,0:T(8,128)(2,1)S(1)} %collective-permute-done.22.rest_5_), channel_id=1, source_target_pairs={{0,4},{1,13},{2,6},{3,15},{4,8},{5,1},{6,10},{7,3},{8,12},{9,5},{1... | collective-permute-start | bytes 1179656 | tf_op jit(solution)/shard_map/f_from1b/ppermute | solution.py:96
  116.9 9.2 %collective-permute-start.31 = (bf16[16,16,768]{2,1,0:T(8,128)(2,1)S(1)}, bf16[16,16,768]{2,1,0:T(8,128)(2,1)S(1)}, u32[]{:S(2)}, u32[]{:S(2)}) collective-permute-start(bf16[16,16,768]{2,1,0:T(8,128)(2,1)S(1)} %collective-permute-done.26.rest_0_), channel_id=1, source_target_pairs={{0,4},{1,13},{2,6},{3,15},{4,8},{5,1},{6,10},{7,3},{8,12},{9,5},{1... | collective-permute-start | bytes 1179656 | tf_op jit(solution)/shard_map/g_from3a/ppermute | solution.py:96
  118.3 11.8 %collective-permute-start.30 = (bf16[16,16,768]{2,1,0:T(8,128)(2,1)S(1)}, bf16[16,16,768]{2,1,0:T(8,128)(2,1)S(1)}, u32[]{:S(2)}, u32[]{:S(2)}) collective-permute-start(bf16[16,16,768]{2,1,0:T(8,128)(2,1)S(1)} %collective-permute-done.25.rest_1_), channel_id=1, source_target_pairs={{0,4},{1,13},{2,6},{3,15},{4,8},{5,1},{6,10},{7,3},{8,12},{9,5},{1... | collective-permute-start | bytes 1179656 | tf_op jit(solution)/shard_map/g_from3b/ppermute | solution.py:96
  126.1 9.6 %collective-permute-start.36 = (bf16[16,16,768]{2,1,0:T(8,128)(2,1)S(1)}, bf16[16,16,768]{2,1,0:T(8,128)(2,1)S(1)}, u32[]{:S(2)}, u32[]{:S(2)}) collective-permute-start(bf16[16,16,768]{2,1,0:T(8,128)(2,1)S(1)} %collective-permute-done.31.rest_6_), channel_id=1, source_target_pairs={{0,4},{1,13},{2,6},{3,15},{4,8},{5,1},{6,10},{7,3},{8,12},{9,5},{1... | collective-permute-start | bytes 1179656 | tf_op jit(solution)/shard_map/g_from2a/ppermute | solution.py:96
  126.4 3.9 %collective-permute-start.29 = (bf16[416,384]{1,0:T(8,128)(2,1)S(1)}, bf16[416,384]{1,0:T(8,128)(2,1)S(1)}, u32[]{:S(2)}, u32[]{:S(2)}) collective-permute-start(bf16[416,384]{1,0:T(8,128)(2,1)S(1)} %get-tuple-element.468), channel_id=1, source_target_pairs={{0,1},{1,0},{2,3},{3,2},{4,5},{5,4},{6,7},{7,6},{8,9},{9,8},{10,11... | collective-permute-start | bytes 958472 | tf_op jit(solution)/shard_map/sum_core/ppermute | solution.py:105
  130.1 9.3 %collective-permute-start.35 = (bf16[16,16,768]{2,1,0:T(8,128)(2,1)S(1)}, bf16[16,16,768]{2,1,0:T(8,128)(2,1)S(1)}, u32[]{:S(2)}, u32[]{:S(2)}) collective-permute-start(bf16[16,16,768]{2,1,0:T(8,128)(2,1)S(1)} %collective-permute-done.30.rest_7_), channel_id=1, source_target_pairs={{0,4},{1,13},{2,6},{3,15},{4,8},{5,1},{6,10},{7,3},{8,12},{9,5},{1... | collective-permute-start | bytes 1179656 | tf_op jit(solution)/shard_map/g_from2b/ppermute | solution.py:96
  131.0 8.5 %collective-permute-start.32 = (bf16[104,384]{1,0:T(8,128)(2,1)S(1)}, bf16[104,384]{1,0:T(8,128)(2,1)S(1)}, u32[]{:S(2)}, u32[]{:S(2)}) collective-permute-start(bf16[104,384]{1,0:T(8,128)(2,1)S(1)} %get-tuple-element.486), channel_id=1, source_target_pairs={{0,32},{1,33},{2,34},{3,35},{4,36},{5,37},{6,38},{7,39},{8,40},{9,... | collective-permute-start | bytes 239624 | tf_op jit(solution)/shard_map/sum_y/ppermute | solution.py:105
  132.6 6.8 %collective-permute-start.33 = (bf16[104,384]{1,0:T(8,128)(2,1)S(1)}, bf16[104,384]{1,0:T(8,128)(2,1)S(1)}, u32[]{:S(2)}, u32[]{:S(2)}) collective-permute-start(bf16[104,384]{1,0:T(8,128)(2,1)S(1)} %get-tuple-element.487), channel_id=1, source_target_pairs={{0,64},{1,65},{2,66},{3,67},{4,68},{5,69},{6,70},{7,71},{8,72},{9,... | collective-permute-start | bytes 239624 | tf_op jit(solution)/shard_map/sum_y/ppermute | solution.py:105
  135.5 5.6 %collective-permute-start.34 = (bf16[104,384]{1,0:T(8,128)(2,1)S(1)}, bf16[104,384]{1,0:T(8,128)(2,1)S(1)}, u32[]{:S(2)}, u32[]{:S(2)}) collective-permute-start(bf16[104,384]{1,0:T(8,128)(2,1)S(1)} %get-tuple-element.488), channel_id=1, source_target_pairs={{0,96},{1,97},{2,98},{3,99},{4,100},{5,101},{6,102},{7,103},{8,104... | collective-permute-start | bytes 239624 | tf_op jit(solution)/shard_map/sum_y/ppermute | solution.py:105
  135.7 9.0 %collective-permute-start.38 = (bf16[16,16,768]{2,1,0:T(8,128)(2,1)S(1)}, bf16[16,16,768]{2,1,0:T(8,128)(2,1)S(1)}, u32[]{:S(2)}, u32[]{:S(2)}) collective-permute-start(bf16[16,16,768]{2,1,0:T(8,128)(2,1)S(1)} %collective-permute-done.36.rest_4_), channel_id=1, source_target_pairs={{0,4},{1,13},{2,6},{3,15},{4,8},{5,1},{6,10},{7,3},{8,12},{9,5},{1... | collective-permute-start | bytes 1179656 | tf_op jit(solution)/shard_map/g_from1a/ppermute | solution.py:96
  139.4 9.5 %collective-permute-start.40 = (bf16[16,16,768]{2,1,0:T(8,128)(2,1)S(1)}, bf16[16,16,768]{2,1,0:T(8,128)(2,1)S(1)}, u32[]{:S(2)}, u32[]{:S(2)}) collective-permute-start(bf16[16,16,768]{2,1,0:T(8,128)(2,1)S(1)} %collective-permute-done.35.rest_5_), channel_id=1, source_target_pairs={{0,4},{1,13},{2,6},{3,15},{4,8},{5,1},{6,10},{7,3},{8,12},{9,5},{1... | collective-permute-start | bytes 1179656 | tf_op jit(solution)/shard_map/g_from1b/ppermute | solution.py:96
  141.2 4.5 %collective-permute-start.37 = (bf16[104,384]{1,0:T(8,128)(2,1)S(1)}, bf16[104,384]{1,0:T(8,128)(2,1)S(1)}, u32[]{:S(2)}, u32[]{:S(2)}) collective-permute-start(bf16[104,384]{1,0:T(8,128)(2,1)S(1)} %add_convert_fusion.16), channel_id=1, source_target_pairs={{0,16},{1,17},{2,18},{3,19},{4,20},{5,21},{6,22},{7,23},{8,24},{9,... | collective-permute-start | bytes 239624 | tf_op jit(solution)/shard_map/sum_x1/ppermute | solution.py:105
  141.3 23.8 %collective-permute-start.28 = (bf16[8,11,16,768]{3,2,1,0:T(8,128)(2,1)}, bf16[8,11,16,768]{3,2,1,0:T(8,128)(2,1)S(1)}, u32[]{:S(2)}, u32[]{:S(2)}) collective-permute-start(bf16[8,11,16,768]{3,2,1,0:T(8,128)(2,1)} %get-tuple-element.466), channel_id=1, source_target_pairs={{0,1},{1,0},{2,3},{3,2},{4,5},{5,4},{6,7},{7,6},{8,9},{9,8},{10,11... | collective-permute-start | bytes 6488072 | tf_op jit(solution)/shard_map/f_pair_back/ppermute | solution.py:105
  145.7 6.0 %collective-permute-start.39 = (bf16[104,384]{1,0:T(8,128)(2,1)S(1)}, bf16[104,384]{1,0:T(8,128)(2,1)S(1)}, u32[]{:S(2)}, u32[]{:S(2)}) collective-permute-start(bf16[104,384]{1,0:T(8,128)(2,1)S(1)} %add_convert_fusion.15), channel_id=1, source_target_pairs={{0,2},{1,3},{2,0},{3,1},{4,6},{5,7},{6,4},{7,5},{8,10},{9,11},{10,... | collective-permute-start | bytes 239624 | tf_op jit(solution)/shard_map/sum_x2/ppermute | solution.py:105
  156.6 21.5 %collective-permute-start.42 = (bf16[8,11,16,768]{3,2,1,0:T(8,128)(2,1)}, bf16[8,11,16,768]{3,2,1,0:T(8,128)(2,1)}, u32[]{:S(2)}, u32[]{:S(2)}) collective-permute-start(bf16[8,11,16,768]{3,2,1,0:T(8,128)(2,1)} %get-tuple-element.524), channel_id=1, source_target_pairs={{0,1},{1,0},{2,3},{3,2},{4,5},{5,4},{6,7},{7,6},{8,9},{9,8},{10,11... | collective-permute-start | bytes 6488072 | tf_op jit(solution)/shard_map/g_pair_back/ppermute | solution.py:105
  156.6 4.8 %collective-permute-start.41 = (bf16[104,384]{1,0:T(8,128)(2,1)S(1)}, bf16[104,384]{1,0:T(8,128)(2,1)S(1)}, u32[]{:S(2)}, u32[]{:S(2)}) collective-permute-start(bf16[104,384]{1,0:T(8,128)(2,1)S(1)} %add_convert_fusion.14), channel_id=1, source_target_pairs={{0,4},{1,5},{2,6},{3,7},{4,0},{5,1},{6,2},{7,3},{8,12},{9,13},{10,... | collective-permute-start | bytes 239624 | tf_op jit(solution)/shard_map/sum_z1/ppermute | solution.py:105
  161.4 10.5 %collective-permute-start.43 = (bf16[104,384]{1,0:T(8,128)(2,1)S(1)}, bf16[104,384]{1,0:T(8,128)(2,1)S(1)}, u32[]{:S(2)}, u32[]{:S(2)}) collective-permute-start(bf16[104,384]{1,0:T(8,128)(2,1)S(1)} %add_convert_fusion.13), channel_id=1, source_target_pairs={{0,8},{1,9},{2,10},{3,11},{4,12},{5,13},{6,14},{7,15},{8,0},{9,1},... | collective-permute-start | bytes 239624 | tf_op jit(solution)/shard_map/sum_z2/ppermute | solution.py:105
  171.9 1.4 collective-permute-start.44
  173.3 15.6 %collective-permute-start.45 = (bf16[2,104,384]{2,1,0:T(8,128)(2,1)S(1)}, bf16[2,104,384]{2,1,0:T(8,128)(2,1)S(1)}, u32[]{:S(2)}, u32[]{:S(2)}) collective-permute-start(bf16[2,104,384]{2,1,0:T(8,128)(2,1)S(1)} %pad_maximum_fusion.p0), channel_id=1, source_target_pairs={{0,32},{1,33},{2,34},{3,35},{4,36},{5,37},{6,38},{7,39},{8,40},{9,... | collective-permute-start | bytes 479240 | tf_op jit(solution)/shard_map/all_y/ppermute | solution.py:105
  173.4 15.5 %collective-permute-start.46 = (bf16[2,104,384]{2,1,0:T(8,128)(2,1)S(1)}, bf16[2,104,384]{2,1,0:T(8,128)(2,1)S(1)}, u32[]{:S(2)}, u32[]{:S(2)}) collective-permute-start(bf16[2,104,384]{2,1,0:T(8,128)(2,1)S(1)} %pad_maximum_fusion.p0), channel_id=1, source_target_pairs={{0,64},{1,65},{2,66},{3,67},{4,68},{5,69},{6,70},{7,71},{8,72},{9,... | collective-permute-start | bytes 479240 | tf_op jit(solution)/shard_map/all_y/ppermute | solution.py:105
  176.2 12.7 %collective-permute-start.47 = (bf16[2,104,384]{2,1,0:T(8,128)(2,1)S(1)}, bf16[2,104,384]{2,1,0:T(8,128)(2,1)S(1)}, u32[]{:S(2)}, u32[]{:S(2)}) collective-permute-start(bf16[2,104,384]{2,1,0:T(8,128)(2,1)S(1)} %pad_maximum_fusion.p0), channel_id=1, source_target_pairs={{0,96},{1,97},{2,98},{3,99},{4,100},{5,101},{6,102},{7,103},{8,104... | collective-permute-start | bytes 479240 | tf_op jit(solution)/shard_map/all_y/ppermute | solution.py:105
  (27 other events, 333.0 us)
where the time goes:
time: 192 us; the launch traced here: 191 us
  Pallas kernels  69.6 us (36%)
  waiting for transfers between devices  66 us (34%)
  starting transfers between devices  45.4 us (24%)
  other arithmetic  5.64 us (3%)
  between operations  2.56 us (1%)
  local copies, waits for them, and re-layouts  2.12 us (1%)
    ppermute x24, waiting for transfers between devices, onward(): return lax.ppermute(array, AXES, pairs)  40.7 us
    ppermute x24, starting transfers between devices, onward(): return lax.ppermute(array, AXES, pairs)  20.4 us
    ppermute x16, starting transfers between devices, swap(): return lax.ppermute(array, AXES, pairs)  14.4 us
    pallas_call x2, Pallas kernels, lon_forward(): call(kernel, 'lon_forward', (ROWS // step,), specs, [row_block(step, COLS...  13.8 us
    ppermute x8, waiting for transfers between devices, shift(): return lax.ppermute(array, AXES, pairs)  13.7 us
    pallas_call x2, Pallas kernels, lat_forward(): call(kernel, 'lat_forward', (C // LANES,), lat_tables((KH * 2 * WB, ROWS...  13.5 us
    ppermute x16, waiting for transfers between devices, swap(): return lax.ppermute(array, AXES, pairs)  11.5 us
    pallas_call x1, Pallas kernels, lon_inverse_grad(): call(kernel, 'lon_inverse_grad', (ROWS // step,), [own_table((W, KW)), be...  10.8 us
  transfers between devices with their start and end apart: 48, of which 26 were waited for; matrix products, arithmetic and copies ran while one was open for 3% of the time, Pallas kernels for 31%

commit v1 on v0

--- a/solution.py
+++ b/solution.py
@@ -204,7 +204,7 @@
     ]
 
 
-LANES = 256
+LANES = 384
 
 
 def slot_base(info, step, half, owned):

time: 192 us -> 205 us (1.068); the launches traced: 191 us -> 201 us
  starting transfers between devices: 45.4 us -> 56 us
    ppermute x8, starting transfers between devices: 10.6 us -> 20.4 us  [shift(): return lax.ppermute(array, AXES, pairs)]
  transfers between devices with their start and end apart: 48 -> 48, of which waited for: 26 -> 27; matrix products, arithmetic and copies ran while one was open for 3% -> 3% of each run, Pallas kernels for 31% -> 29%
where the time goes in v1:
time: 205 us; the launch traced here: 201 us
  Pallas kernels  67.7 us (33%)
  waiting for transfers between devices  66.7 us (33%)
  starting transfers between devices  56 us (27%)
  other arithmetic  5.64 us (3%)
  between operations  2.74 us (1%)
  local copies, waits for them, and re-layouts  2.12 us (1%)
    ppermute x24, waiting for transfers between devices, onward(): return lax.ppermute(array, AXES, pairs)  40.4 us
    ppermute x24, starting transfers between devices, onward(): return lax.ppermute(array, AXES, pairs)  20.8 us
    ppermute x8, starting transfers between devices, shift(): return lax.ppermute(array, AXES, pairs)  20.4 us
    ppermute x8, waiting for transfers between devices, shift(): return lax.ppermute(array, AXES, pairs)  14.8 us
    ppermute x16, starting transfers between devices, swap(): return lax.ppermute(array, AXES, pairs)  14.8 us
    pallas_call x2, Pallas kernels, lon_forward(): call(kernel, 'lon_forward', (ROWS // step,), specs, [row_block(step, COLS...  13.8 us
    pallas_call x2, Pallas kernels, lat_forward(): call(kernel, 'lat_forward', (C // LANES,), lat_tables((KH * 2 * WB, ROWS...  11.6 us
    ppermute x16, waiting for transfers between devices, swap(): return lax.ppermute(array, AXES, pairs)  11.4 us
  transfers between devices with their start and end apart: 48, of which 27 were waited for; matrix products, arithmetic and copies ran while one was open for 3% of the time, Pallas kernels for 29%

profile of v1, /device:TPU:6, one launch (start us, length us, event | category | flops | bytes accessed | tf_op | source)
XLA Modules:
  0.0 200.8 jit_solution(1547157536007305721)
XLA Ops:
  1.9 7.7 %lon_forward.2 = (bf16[8,11,16,768]{3,2,1,0:T(8,128)(2,1)}, bf16[8,11,16,768]{3,2,1,0:T(8,128)(2,1)}) custom-call(s32[8]{0:T(128)S(1)} %stack.58.info, s32[176]{0:T(256)S(1)} %convert_reduce_fusion.slots, s32[16]{0:T(128)} %cuts.27, bf16[2,176,360]{2,1,0:T(8,128)(2,1)} %constant.127.clone.own_t.beside_t, ...), custom_call_target="tpu_custom_call" | custom-call | tf_op jit(solution)/shard_map/lon_forward/pallas_call | solution.py:182
  9.6 6.1 %lon_forward.3 = (bf16[8,11,16,768]{3,2,1,0:T(8,128)(2,1)}, bf16[8,11,16,768]{3,2,1,0:T(8,128)(2,1)}) custom-call(s32[8]{0:T(128)S(1)} %stack.58.info, s32[176]{0:T(256)S(1)} %convert_reduce_fusion.slots, s32[16]{0:T(128)S(1)} %copy-done.12, bf16[2,176,360]{2,1,0:T(8,128)(2,1)} %constant.128.clone.own_t.beside_t, ...), custom_call_target="tpu_custom_call" | custom-call | tf_op jit(solution)/shard_map/lon_forward/pallas_call | solution.py:182
  16.2 5.8 %lat_forward.2 = (bf16[16,16,768]{2,1,0:T(8,128)(2,1)}, bf16[16,16,768]{2,1,0:T(8,128)(2,1)}, bf16[16,16,768]{2,1,0:T(8,128)(2,1)}, bf16[16,16,768]{2,1,0:T(8,12...) custom-call(s32[8]{0:T(128)S(1)} %stack.58.info, ...), custom_call_target="tpu_custom_call" | custom-call | tf_op jit(solution)/shard_map/lat_forward/pallas_call | solution.py:236
  22.0 2.0 collective-permute-start.3
  24.0 1.9 collective-permute-start.2
  25.9 5.8 %lat_forward.3 = (bf16[16,16,768]{2,1,0:T(8,128)(2,1)}, bf16[16,16,768]{2,1,0:T(8,128)(2,1)}, bf16[16,16,768]{2,1,0:T(8,128)(2,1)}, bf16[16,16,768]{2,1,0:T(8,12...) custom-call(s32[8]{0:T(128)S(1)} %stack.58.info, ...), custom_call_target="tpu_custom_call" | custom-call | tf_op jit(solution)/shard_map/lat_forward/pallas_call | solution.py:236
  33.5 2.7 %collective-permute-done.2 = bf16[16,16,768]{2,1,0:T(8,128)(2,1)S(1)} collective-permute-done((bf16[16,16,768]{2,1,0:T(8,128)(2,1)}, bf16[16,16,768]{2,1,0:T(8,128)(2,1)S(1)}, u32[]{:S(2)}, u32[]{:S(2)}) %collective-permute-start.2) | collective-permute-done | bytes 393248 | tf_op jit(solution)/shard_map/f3b/ppermute | solution.py:96
  36.5 1.8 wide_weights.1.rest_1_.rest_2_
  38.3 2.9 %collective-permute-done.5 = bf16[16,16,768]{2,1,0:T(8,128)(2,1)S(1)} collective-permute-done((bf16[16,16,768]{2,1,0:T(8,128)(2,1)S(1)}, bf16[16,16,768]{2,1,0:T(8,128)(2,1)S(1)}, u32[]{:S(2)}, u32[]{:S(2)}) %collective-permute-start.5) | collective-permute-done | bytes 393248 | tf_op jit(solution)/shard_map/f2a/ppermute | solution.py:96
  41.5 3.9 %collective-permute-done.4 = bf16[16,16,768]{2,1,0:T(8,128)(2,1)S(1)} collective-permute-done((bf16[16,16,768]{2,1,0:T(8,128)(2,1)S(1)}, bf16[16,16,768]{2,1,0:T(8,128)(2,1)S(1)}, u32[]{:S(2)}, u32[]{:S(2)}) %collective-permute-start.4) | collective-permute-done | bytes 393248 | tf_op jit(solution)/shard_map/f2b/ppermute | solution.py:96
  45.7 4.7 %collective-permute-done.7 = bf16[16,16,768]{2,1,0:T(8,128)(2,1)S(1)} collective-permute-done((bf16[16,16,768]{2,1,0:T(8,128)(2,1)S(1)}, bf16[16,16,768]{2,1,0:T(8,128)(2,1)S(1)}, u32[]{:S(2)}, u32[]{:S(2)}) %collective-permute-start.7) | collective-permute-done | bytes 393248 | tf_op jit(solution)/shard_map/f1a/ppermute | solution.py:96
  50.6 4.0 %collective-permute-done.6 = bf16[16,16,768]{2,1,0:T(8,128)(2,1)S(1)} collective-permute-done((bf16[16,16,768]{2,1,0:T(8,128)(2,1)S(1)}, bf16[16,16,768]{2,1,0:T(8,128)(2,1)S(1)}, u32[]{:S(2)}, u32[]{:S(2)}) %collective-permute-start.6) | collective-permute-done | bytes 393248 | tf_op jit(solution)/shard_map/f1b/ppermute | solution.py:96
  55.2 1.6 collective-permute-start.9
  56.9 2.7 %collective-permute-done.11 = bf16[16,16,768]{2,1,0:T(8,128)(2,1)S(1)} collective-permute-done((bf16[16,16,768]{2,1,0:T(8,128)(2,1)S(1)}, bf16[16,16,768]{2,1,0:T(8,128)(2,1)S(1)}, u32[]{:S(2)}, u32[]{:S(2)}) %collective-permute-start.11) | collective-permute-done | bytes 393248 | tf_op jit(solution)/shard_map/g3a/ppermute | solution.py:96
  59.7 3.2 %collective-permute-done.10.xl = bf16[16,16,768]{2,1,0:T(8,128)(2,1)S(1)} collective-permute-done((bf16[16,16,768]{2,1,0:T(8,128)(2,1)S(1)}, bf16[16,16,768]{2,1,0:T(8,128)(2,1)S(1)}, u32[]{:S(2)}, u32[]{:S(2)}) %collective-permute-start.10) | collective-permute-done | bytes 393248 | tf_op jit(solution)/shard_map/f_left/ppermute | solution.py:87
  67.2 2.4 %spectral_forward.3 = (bf16[16,16,768]{2,1,0:T(8,128)(2,1)S(1)}, bf16[2,128,768]{2,1,0:T(8,128)(2,1)S(1)}, bf16[2,128,768]{2,1,0:T(8,128)(2,1)S(1)}, f32[2,128,768]{2,1,0:T(8,128)S(1)}) custom-call(s32[8]{0:T(128)S(1)} %stack.58.info, s32[176]{0:T(256)S(1)} %convert_reduce_fusion.slots, s32[16]{0:T(128)S(1)} %copy-done.12, ...), custom_call_target="tpu_custom_call" | custom-call | tf_op jit(solution)/shard_map/spectral_forward/pallas_call | solution.py:453
  70.8 2.9 %collective-permute-start.12 = (bf16[16,16,768]{2,1,0:T(8,128)(2,1)S(1)}, bf16[16,16,768]{2,1,0:T(8,128)(2,1)}, u32[]{:S(2)}, u32[]{:S(2)}) collective-permute-start(bf16[16,16,768]{2,1,0:T(8,128)(2,1)S(1)} %get-tuple-element.392), channel_id=1, source_target_pairs={{0,16},{1,17},{2,18},{3,19},{4,20},{5,21},{6,22},{7,23},{8,24},{9,... | collective-permute-start | bytes 1179656 | tf_op jit(solution)/shard_map/f_back_b/ppermute | solution.py:87
  74.0 2.4 %collective-permute-start.18 = (bf16[16,16,768]{2,1,0:T(8,128)(2,1)S(1)}, bf16[16,16,768]{2,1,0:T(8,128)(2,1)S(1)}, u32[]{:S(2)}, u32[]{:S(2)}) collective-permute-start(bf16[16,16,768]{2,1,0:T(8,128)(2,1)S(1)} %add_convert_fusion.3), channel_id=1, source_target_pairs={{0,4},{1,13},{2,6},{3,15},{4,8},{5,1},{6,10},{7,3},{8,12},{9,5},{1... | collective-permute-start | bytes 1179656 | tf_op jit(solution)/shard_map/g1a/ppermute | solution.py:96
  76.4 1.7 collective-permute-done.14
  80.3 2.3 %collective-permute-done.13.rest_0_ = bf16[16,16,768]{2,1,0:T(8,128)(2,1)} collective-permute-done((bf16[16,16,768]{2,1,0:T(8,128)(2,1)S(1)}, bf16[16,16,768]{2,1,0:T(8,128)(2,1)}, u32[]{:S(2)}, u32[]{:S(2)}) %collective-permute-start.13) | collective-permute-done | bytes 393248 | tf_op jit(solution)/shard_map/f_back_a/ppermute | solution.py:87
  82.6 1.7 collective-permute-start.21
  85.2 2.2 %collective-permute-done.17 = bf16[16,16,768]{2,1,0:T(8,128)(2,1)} collective-permute-done((bf16[16,16,768]{2,1,0:T(8,128)(2,1)S(1)}, bf16[16,16,768]{2,1,0:T(8,128)(2,1)}, u32[]{:S(2)}, u32[]{:S(2)}) %collective-permute-start.17) | collective-permute-done | bytes 393248 | tf_op jit(solution)/shard_map/g1b/ppermute | solution.py:96
  87.4 1.9 add_convert_fusion
  93.6 3.9 %collective-permute-done.20.xl = bf16[16,16,768]{2,1,0:T(8,128)(2,1)} collective-permute-done((bf16[16,16,768]{2,1,0:T(8,128)(2,1)}, bf16[16,16,768]{2,1,0:T(8,128)(2,1)}, u32[]{:S(2)}, u32[]{:S(2)}) %collective-permute-start.20) | collective-permute-done | bytes 393248 | tf_op jit(solution)/shard_map/g_left/ppermute | solution.py:87
  97.6 1.7 collective-permute-done.19.rest_0_
  100.9 4.4 %spectral_backward.3 = (bf16[16,16,768]{2,1,0:T(8,128)(2,1)S(1)}, bf16[2,128,768]{2,1,0:T(8,128)(2,1)S(1)}, bf16[2,128,768]{2,1,0:T(8,128)(2,1)S(1)}, f32[2,8,768]{2,1,0:T(8,128)S(1)}) custom-call(s32[8]{0:T(128)S(1)} %get-tuple-element.649, s32[176]{0:T(256)S(1)} %get-tuple-element.650, s32[16]{0:T(128)S(1)} %get-tuple-element.651, ...), custom_call_target="tpu_custom_call" | custom-call | tf_op jit(solution)/shard_map/spectral_backward/pallas_call | solution.py:486
  105.4 1.8 collective-permute-start.27
  107.1 9.8 %collective-permute-start.26 = (bf16[16,16,768]{2,1,0:T(8,128)(2,1)S(1)}, bf16[16,16,768]{2,1,0:T(8,128)(2,1)S(1)}, u32[]{:S(2)}, u32[]{:S(2)}) collective-permute-start(bf16[16,16,768]{2,1,0:T(8,128)(2,1)S(1)} %get-tuple-element.446), channel_id=1, source_target_pairs={{0,18},{1,19},{2,16},{3,17},{4,22},{5,23},{6,20},{7,21},{8,26},{9,... | collective-permute-start | bytes 1179656 | tf_op jit(solution)/shard_map/g_back_a/ppermute | solution.py:87
  117.0 3.2 %collective-permute-start.25 = (bf16[16,16,768]{2,1,0:T(8,128)(2,1)S(1)}, bf16[16,16,768]{2,1,0:T(8,128)(2,1)S(1)}, u32[]{:S(2)}, u32[]{:S(2)}) collective-permute-start(bf16[16,16,768]{2,1,0:T(8,128)(2,1)S(1)} %get-tuple-element.446), channel_id=1, source_target_pairs={{0,16},{1,17},{2,18},{3,19},{4,20},{5,21},{6,22},{7,23},{8,24},{9,... | collective-permute-start | bytes 1179656 | tf_op jit(solution)/shard_map/g_back_b/ppermute | solution.py:87
  121.5 2.3 %weight_sums.3 = (bf16[416,384]{1,0:T(8,128)(2,1)S(1)}, f32[416,384]{1,0:T(8,128)S(1)}) custom-call(s32[8]{0:T(128)S(1)} %get-tuple-element.649, s32[176]{0:T(256)S(1)} %get-tuple-element.650, s32[16]{0:T(128)S(1)} %get-tuple-element.651, bf16[2,128,768]{2,1,0:T(8,128)(2,1)S(1)} %get-tuple-element.437.rest_3_.u0, ...), custom_call_target="tpu_custom_call" | custom-call | tf_op jit(solution)/shard_map/weight_sums/pallas_call | solution.py:542
  123.8 2.1 %collective-permute-done.26.rest_0_ = bf16[16,16,768]{2,1,0:T(8,128)(2,1)S(1)} collective-permute-done((bf16[16,16,768]{2,1,0:T(8,128)(2,1)S(1)}, bf16[16,16,768]{2,1,0:T(8,128)(2,1)S(1)}, u32[]{:S(2)}, u32[]{:S(2)}) %collective-permute-start.26) | collective-permute-done | bytes 393248 | tf_op jit(solution)/shard_map/g_back_a/ppermute | solution.py:87
  129.2 5.7 %lat_inverse.2 = (bf16[8,11,16,768]{3,2,1,0:T(8,128)(2,1)}, bf16[8,11,16,768]{3,2,1,0:T(8,128)(2,1)}) custom-call(s32[8]{0:T(128)S(1)} %get-tuple-element.649, s32[176]{0:T(256)S(1)} %get-tuple-element.650, s32[16]{0:T(128)S(1)} %get-tuple-element.651, bf16[16,128,256]{2,1,0:T(8,128)(2,1)S(1)} %copy-done.1, bf16[16,128,256]{2,1,0:T(8,128)(2,1)S(1)} %copy-done.1, ...), custom_call_target="tpu_custom_call" | custom-call | tf_op jit(solution)/shard_map/lat_inverse/pallas_call | solution.py:273
  135.1 4.1 %collective-permute-done.30.rest_7_ = bf16[16,16,768]{2,1,0:T(8,128)(2,1)S(1)} collective-permute-done((bf16[16,16,768]{2,1,0:T(8,128)(2,1)S(1)}, bf16[16,16,768]{2,1,0:T(8,128)(2,1)S(1)}, u32[]{:S(2)}, u32[]{:S(2)}) %collective-permute-start.30) | collective-permute-done | bytes 393248 | tf_op jit(solution)/shard_map/g_from3b/ppermute | solution.py:96
  139.9 1.7 collective-permute-start.32
  141.5 2.9 %collective-permute-start.33 = (bf16[104,384]{1,0:T(8,128)(2,1)S(1)}, bf16[104,384]{1,0:T(8,128)(2,1)S(1)}, u32[]{:S(2)}, u32[]{:S(2)}) collective-permute-start(bf16[104,384]{1,0:T(8,128)(2,1)S(1)} %get-tuple-element.487), channel_id=1, source_target_pairs={{0,64},{1,65},{2,66},{3,67},{4,68},{5,69},{6,70},{7,71},{8,72},{9,... | collective-permute-start | bytes 239624 | tf_op jit(solution)/shard_map/sum_y/ppermute | solution.py:105
  145.0 3.1 %collective-permute-done.35.rest_5_ = bf16[16,16,768]{2,1,0:T(8,128)(2,1)S(1)} collective-permute-done((bf16[16,16,768]{2,1,0:T(8,128)(2,1)S(1)}, bf16[16,16,768]{2,1,0:T(8,128)(2,1)S(1)}, u32[]{:S(2)}, u32[]{:S(2)}) %collective-permute-start.35) | collective-permute-done | bytes 393248 | tf_op jit(solution)/shard_map/g_from2b/ppermute | solution.py:96
  148.2 1.9 collective-permute-done.34
  150.3 3.3 %collective-permute-done.38.rest_2_ = bf16[16,16,768]{2,1,0:T(8,128)(2,1)S(1)} collective-permute-done((bf16[16,16,768]{2,1,0:T(8,128)(2,1)S(1)}, bf16[16,16,768]{2,1,0:T(8,128)(2,1)S(1)}, u32[]{:S(2)}, u32[]{:S(2)}) %collective-permute-start.38) | collective-permute-done | bytes 393248 | tf_op jit(solution)/shard_map/g_from1a/ppermute | solution.py:96
  155.1 2.8 %collective-permute-done.40.rest_3_ = bf16[16,16,768]{2,1,0:T(8,128)(2,1)S(1)} collective-permute-done((bf16[16,16,768]{2,1,0:T(8,128)(2,1)S(1)}, bf16[16,16,768]{2,1,0:T(8,128)(2,1)S(1)}, u32[]{:S(2)}, u32[]{:S(2)}) %collective-permute-start.40) | collective-permute-done | bytes 393248 | tf_op jit(solution)/shard_map/g_from1b/ppermute | solution.py:96
  157.9 2.8 %collective-permute-done.39 = bf16[104,384]{1,0:T(8,128)(2,1)S(1)} collective-permute-done((bf16[104,384]{1,0:T(8,128)(2,1)S(1)}, bf16[104,384]{1,0:T(8,128)(2,1)S(1)}, u32[]{:S(2)}, u32[]{:S(2)}) %collective-permute-start.39) | collective-permute-done | bytes 79904 | tf_op jit(solution)/shard_map/sum_x2/ppermute | solution.py:105
  160.7 5.1 %lat_inverse.3 = (bf16[8,11,16,768]{3,2,1,0:T(8,128)(2,1)}, bf16[8,11,16,768]{3,2,1,0:T(8,128)(2,1)}) custom-call(s32[8]{0:T(128)S(1)} %get-tuple-element.649, s32[176]{0:T(256)S(1)} %get-tuple-element.650, s32[16]{0:T(128)S(1)} %get-tuple-element.651, bf16[16,128,256]{2,1,0:T(8,128)(2,1)S(1)} %copy-done.1, bf16[16,128,256]{2,1,0:T(8,128)(2,1)S(1)} %copy-done.1, ...), custom_call_target="tpu_custom_call" | custom-call | tf_op jit(solution)/shard_map/lat_inverse/pallas_call | solution.py:273
  166.2 4.5 %collective-permute-done.41 = bf16[104,384]{1,0:T(8,128)(2,1)S(1)} collective-permute-done((bf16[104,384]{1,0:T(8,128)(2,1)S(1)}, bf16[104,384]{1,0:T(8,128)(2,1)S(1)}, u32[]{:S(2)}, u32[]{:S(2)}) %collective-permute-start.41) | collective-permute-done | bytes 79904 | tf_op jit(solution)/shard_map/sum_z1/ppermute | solution.py:105
  170.7 3.7 %collective-permute-start.43 = (bf16[104,384]{1,0:T(8,128)(2,1)S(1)}, bf16[104,384]{1,0:T(8,128)(2,1)S(1)}, u32[]{:S(2)}, u32[]{:S(2)}) collective-permute-start(bf16[104,384]{1,0:T(8,128)(2,1)S(1)} %add_convert_fusion.13), channel_id=1, source_target_pairs={{0,8},{1,9},{2,10},{3,11},{4,12},{5,13},{6,14},{7,15},{8,0},{9,1},... | collective-permute-start | bytes 239624 | tf_op jit(solution)/shard_map/sum_z2/ppermute | solution.py:105
  174.4 6.8 %lon_inverse_fields.1 = bf16[8,360,768]{2,1,0:T(8,128)(2,1)} custom-call(s32[8]{0:T(128)S(1)} %get-tuple-element.649, s32[176]{0:T(256)S(1)} %get-tuple-element.650, s32[16]{0:T(128)S(1)} %get-tuple-element.651, bf16[2,360,176]{2,1,0:T(8,128)(2,1)S(1)} %copy-done.3, bf16[2,360,176]{2,1,0:T(8,128)(2,1)S(1)} %copy-done.3, ...), custom_call_target="tpu_custom_call" | custom-call | tf_op jit(solution)/shard_map/lon_inverse_fields/pallas_call | solution.py:300
  182.7 2.6 %collective-permute-start.46 = (bf16[2,104,384]{2,1,0:T(8,128)(2,1)S(1)}, bf16[2,104,384]{2,1,0:T(8,128)(2,1)S(1)}, u32[]{:S(2)}, u32[]{:S(2)}) collective-permute-start(bf16[2,104,384]{2,1,0:T(8,128)(2,1)S(1)} %pad_maximum_fusion.p0), channel_id=1, source_target_pairs={{0,64},{1,65},{2,66},{3,67},{4,68},{5,69},{6,70},{7,71},{8,72},{9,... | collective-permute-start | bytes 479240 | tf_op jit(solution)/shard_map/all_y/ppermute | solution.py:105
  185.3 2.1 %collective-permute-start.47 = (bf16[2,104,384]{2,1,0:T(8,128)(2,1)S(1)}, bf16[2,104,384]{2,1,0:T(8,128)(2,1)S(1)}, u32[]{:S(2)}, u32[]{:S(2)}) collective-permute-start(bf16[2,104,384]{2,1,0:T(8,128)(2,1)S(1)} %pad_maximum_fusion.p0), channel_id=1, source_target_pairs={{0,96},{1,97},{2,98},{3,99},{4,100},{5,101},{6,102},{7,103},{8,104... | collective-permute-start | bytes 479240 | tf_op jit(solution)/shard_map/all_y/ppermute | solution.py:105
  187.4 10.8 %lon_inverse_grad.1 = bf16[8,360,768]{2,1,0:T(8,128)(2,1)} custom-call(s32[8]{0:T(128)S(1)} %get-tuple-element.649, s32[176]{0:T(256)S(1)} %get-tuple-element.650, s32[16]{0:T(128)S(1)} %get-tuple-element.651, bf16[2,360,176]{2,1,0:T(8,128)(2,1)} %constant.125.clone.own_t.beside_t, bf16[2,360,176]{2,1,0:T(8,128)(2,1)} %constant.125.clone.own_t.beside_t, ...), custom_call_target="tpu_custom_call" | custom-call | tf_op jit(solution)/shard_map/lon_inverse_grad/pallas_call | solution.py:327
  198.3 2.4 %place_sums.1 = (f32[2,2,8,96,96]{4,3,2,1,0:T(8,128)}, f32[2,2,768]{2,1,0:T(2,128)}, f32[768]{0:T(1024)}) custom-call(s32[8]{0:T(128)S(1)} %get-tuple-element.649, s32[176]{0:T(256)S(1)} %get-tuple-element.650, s32[16]{0:T(128)S(1)} %get-tuple-element.651, bf16[2,104,384]{2,1,0:T(8,128)(2,1)S(1)} %pad_maximum_fusion.p0, ...), custom_call_target="tpu_custom_call" | custom-call | tf_op jit(solution)/shard_map/place_sums/pallas_call | solution.py:600
  (145 shorter events, 28.2 us)
Async XLA Ops:
  9.6 6.1 %collective-permute-start = (bf16[8,11,16,768]{3,2,1,0:T(8,128)(2,1)}, bf16[8,11,16,768]{3,2,1,0:T(8,128)(2,1)}, u32[]{:S(2)}, u32[]{:S(2)}) collective-permute-start(bf16[8,11,16,768]{3,2,1,0:T(8,128)(2,1)} %get-tuple-element.309), channel_id=1, source_target_pairs={{0,1},{1,0},{2,3},{3,2},{4,5},{5,4},{6,7},{7,6},{8,9},{9,8},{10,11... | collective-permute-start | bytes 6488072 | tf_op jit(solution)/shard_map/f_pair/ppermute | solution.py:105
  15.7 10.2 %collective-permute-start.1 = (bf16[8,11,16,768]{3,2,1,0:T(8,128)(2,1)}, bf16[8,11,16,768]{3,2,1,0:T(8,128)(2,1)}, u32[]{:S(2)}, u32[]{:S(2)}) collective-permute-start(bf16[8,11,16,768]{3,2,1,0:T(8,128)(2,1)} %get-tuple-element.312), channel_id=1, source_target_pairs={{0,1},{1,0},{2,3},{3,2},{4,5},{5,4},{6,7},{7,6},{8,9},{9,8},{10,11... | collective-permute-start | bytes 6488072 | tf_op jit(solution)/shard_map/g_pair/ppermute | solution.py:105
  22.0 10.1 %collective-permute-start.3 = (bf16[16,16,768]{2,1,0:T(8,128)(2,1)}, bf16[16,16,768]{2,1,0:T(8,128)(2,1)S(1)}, u32[]{:S(2)}, u32[]{:S(2)}) collective-permute-start(bf16[16,16,768]{2,1,0:T(8,128)(2,1)} %get-tuple-element.344), channel_id=1, source_target_pairs={{0,4},{1,13},{2,6},{3,15},{4,8},{5,1},{6,10},{7,3},{8,12},{9,5},{1... | collective-permute-start | bytes 1179656 | tf_op jit(solution)/shard_map/f3a/ppermute | solution.py:96
  24.0 12.3 %collective-permute-start.2 = (bf16[16,16,768]{2,1,0:T(8,128)(2,1)}, bf16[16,16,768]{2,1,0:T(8,128)(2,1)S(1)}, u32[]{:S(2)}, u32[]{:S(2)}) collective-permute-start(bf16[16,16,768]{2,1,0:T(8,128)(2,1)} %get-tuple-element.342), channel_id=1, source_target_pairs={{0,4},{1,13},{2,6},{3,15},{4,8},{5,1},{6,10},{7,3},{8,12},{9,5},{1... | collective-permute-start | bytes 1179656 | tf_op jit(solution)/shard_map/f3b/ppermute | solution.py:96
  32.2 9.1 %collective-permute-start.5 = (bf16[16,16,768]{2,1,0:T(8,128)(2,1)S(1)}, bf16[16,16,768]{2,1,0:T(8,128)(2,1)S(1)}, u32[]{:S(2)}, u32[]{:S(2)}) collective-permute-start(bf16[16,16,768]{2,1,0:T(8,128)(2,1)S(1)} %add_convert_fusion.11), channel_id=1, source_target_pairs={{0,4},{1,13},{2,6},{3,15},{4,8},{5,1},{6,10},{7,3},{8,12},{9,5},{1... | collective-permute-start | bytes 1179656 | tf_op jit(solution)/shard_map/f2a/ppermute | solution.py:96
  36.4 9.1 %collective-permute-start.4 = (bf16[16,16,768]{2,1,0:T(8,128)(2,1)S(1)}, bf16[16,16,768]{2,1,0:T(8,128)(2,1)S(1)}, u32[]{:S(2)}, u32[]{:S(2)}) collective-permute-start(bf16[16,16,768]{2,1,0:T(8,128)(2,1)S(1)} %add_convert_fusion.10), channel_id=1, source_target_pairs={{0,4},{1,13},{2,6},{3,15},{4,8},{5,1},{6,10},{7,3},{8,12},{9,5},{1... | collective-permute-start | bytes 1179656 | tf_op jit(solution)/shard_map/f2b/ppermute | solution.py:96
  41.3 9.1 %collective-permute-start.7 = (bf16[16,16,768]{2,1,0:T(8,128)(2,1)S(1)}, bf16[16,16,768]{2,1,0:T(8,128)(2,1)S(1)}, u32[]{:S(2)}, u32[]{:S(2)}) collective-permute-start(bf16[16,16,768]{2,1,0:T(8,128)(2,1)S(1)} %add_convert_fusion.9), channel_id=1, source_target_pairs={{0,4},{1,13},{2,6},{3,15},{4,8},{5,1},{6,10},{7,3},{8,12},{9,5},{1... | collective-permute-start | bytes 1179656 | tf_op jit(solution)/shard_map/f1a/ppermute | solution.py:96
  45.6 9.1 %collective-permute-start.6 = (bf16[16,16,768]{2,1,0:T(8,128)(2,1)S(1)}, bf16[16,16,768]{2,1,0:T(8,128)(2,1)S(1)}, u32[]{:S(2)}, u32[]{:S(2)}) collective-permute-start(bf16[16,16,768]{2,1,0:T(8,128)(2,1)S(1)} %add_convert_fusion.8), channel_id=1, source_target_pairs={{0,4},{1,13},{2,6},{3,15},{4,8},{5,1},{6,10},{7,3},{8,12},{9,5},{1... | collective-permute-start | bytes 1179656 | tf_op jit(solution)/shard_map/f1b/ppermute | solution.py:96
  50.5 9.1 %collective-permute-start.11 = (bf16[16,16,768]{2,1,0:T(8,128)(2,1)S(1)}, bf16[16,16,768]{2,1,0:T(8,128)(2,1)S(1)}, u32[]{:S(2)}, u32[]{:S(2)}) collective-permute-start(bf16[16,16,768]{2,1,0:T(8,128)(2,1)S(1)} %copy-done.27), channel_id=1, source_target_pairs={{0,4},{1,13},{2,6},{3,15},{4,8},{5,1},{6,10},{7,3},{8,12},{9,5},{1... | collective-permute-start | bytes 1179656 | tf_op jit(solution)/shard_map/g3a/ppermute | solution.py:96
  54.6 8.2 %collective-permute-start.10 = (bf16[16,16,768]{2,1,0:T(8,128)(2,1)S(1)}, bf16[16,16,768]{2,1,0:T(8,128)(2,1)S(1)}, u32[]{:S(2)}, u32[]{:S(2)}) collective-permute-start(bf16[16,16,768]{2,1,0:T(8,128)(2,1)S(1)} %add_convert_fusion.7), channel_id=1, source_target_pairs={{0,16},{1,17},{2,18},{3,19},{4,20},{5,21},{6,22},{7,23},{8,24},{9,... | collective-permute-start | bytes 1179656 | tf_op jit(solution)/shard_map/f_left/ppermute | solution.py:87
  55.2 9.2 %collective-permute-start.9 = (bf16[16,16,768]{2,1,0:T(8,128)(2,1)S(1)}, bf16[16,16,768]{2,1,0:T(8,128)(2,1)S(1)}, u32[]{:S(2)}, u32[]{:S(2)}) collective-permute-start(bf16[16,16,768]{2,1,0:T(8,128)(2,1)S(1)} %add_convert_fusion.6), channel_id=1, source_target_pairs={{0,18},{1,19},{2,16},{3,17},{4,22},{5,23},{6,20},{7,21},{8,26},{9,... | collective-permute-start | bytes 1179656 | tf_op jit(solution)/shard_map/f_right/ppermute | solution.py:87
  56.9 9.2 %collective-permute-start.8 = (bf16[16,16,768]{2,1,0:T(8,128)(2,1)S(1)}, bf16[16,16,768]{2,1,0:T(8,128)(2,1)S(1)}, u32[]{:S(2)}, u32[]{:S(2)}) collective-permute-start(bf16[16,16,768]{2,1,0:T(8,128)(2,1)S(1)} %copy-done.26), channel_id=1, source_target_pairs={{0,4},{1,13},{2,6},{3,15},{4,8},{5,1},{6,10},{7,3},{8,12},{9,5},{1... | collective-permute-start | bytes 1179656 | tf_op jit(solution)/shard_map/g3b/ppermute | solution.py:96
  64.4 9.4 %collective-permute-start.15 = (bf16[16,16,768]{2,1,0:T(8,128)(2,1)S(1)}, bf16[16,16,768]{2,1,0:T(8,128)(2,1)S(1)}, u32[]{:S(2)}, u32[]{:S(2)}) collective-permute-start(bf16[16,16,768]{2,1,0:T(8,128)(2,1)S(1)} %add_convert_fusion.5), channel_id=1, source_target_pairs={{0,4},{1,13},{2,6},{3,15},{4,8},{5,1},{6,10},{7,3},{8,12},{9,5},{1... | collective-permute-start | bytes 1179656 | tf_op jit(solution)/shard_map/g2a/ppermute | solution.py:96
  66.2 12.0 %collective-permute-start.14 = (bf16[16,16,768]{2,1,0:T(8,128)(2,1)S(1)}, bf16[16,16,768]{2,1,0:T(8,128)(2,1)S(1)}, u32[]{:S(2)}, u32[]{:S(2)}) collective-permute-start(bf16[16,16,768]{2,1,0:T(8,128)(2,1)S(1)} %add_convert_fusion.4), channel_id=1, source_target_pairs={{0,4},{1,13},{2,6},{3,15},{4,8},{5,1},{6,10},{7,3},{8,12},{9,5},{1... | collective-permute-start | bytes 1179656 | tf_op jit(solution)/shard_map/g2b/ppermute | solution.py:96
  70.5 12.1 %collective-permute-start.13 = (bf16[16,16,768]{2,1,0:T(8,128)(2,1)S(1)}, bf16[16,16,768]{2,1,0:T(8,128)(2,1)}, u32[]{:S(2)}, u32[]{:S(2)}) collective-permute-start(bf16[16,16,768]{2,1,0:T(8,128)(2,1)S(1)} %get-tuple-element.392), channel_id=1, source_target_pairs={{0,18},{1,19},{2,16},{3,17},{4,22},{5,23},{6,20},{7,21},{8,26},{9,... | collective-permute-start | bytes 1179656 | tf_op jit(solution)/shard_map/f_back_a/ppermute | solution.py:87
  70.8 11.8 %collective-permute-start.12 = (bf16[16,16,768]{2,1,0:T(8,128)(2,1)S(1)}, bf16[16,16,768]{2,1,0:T(8,128)(2,1)}, u32[]{:S(2)}, u32[]{:S(2)}) collective-permute-start(bf16[16,16,768]{2,1,0:T(8,128)(2,1)S(1)} %get-tuple-element.392), channel_id=1, source_target_pairs={{0,16},{1,17},{2,18},{3,19},{4,20},{5,21},{6,22},{7,23},{8,24},{9,... | collective-permute-start | bytes 1179656 | tf_op jit(solution)/shard_map/f_back_b/ppermute | solution.py:87
  74.0 10.3 %collective-permute-start.18 = (bf16[16,16,768]{2,1,0:T(8,128)(2,1)S(1)}, bf16[16,16,768]{2,1,0:T(8,128)(2,1)S(1)}, u32[]{:S(2)}, u32[]{:S(2)}) collective-permute-start(bf16[16,16,768]{2,1,0:T(8,128)(2,1)S(1)} %add_convert_fusion.3), channel_id=1, source_target_pairs={{0,4},{1,13},{2,6},{3,15},{4,8},{5,1},{6,10},{7,3},{8,12},{9,5},{1... | collective-permute-start | bytes 1179656 | tf_op jit(solution)/shard_map/g1a/ppermute | solution.py:96
  78.2 9.2 %collective-permute-start.17 = (bf16[16,16,768]{2,1,0:T(8,128)(2,1)S(1)}, bf16[16,16,768]{2,1,0:T(8,128)(2,1)}, u32[]{:S(2)}, u32[]{:S(2)}) collective-permute-start(bf16[16,16,768]{2,1,0:T(8,128)(2,1)S(1)} %add_convert_fusion.2), channel_id=1, source_target_pairs={{0,4},{1,13},{2,6},{3,15},{4,8},{5,1},{6,10},{7,3},{8,12},{9,5},{1... | collective-permute-start | bytes 1179656 | tf_op jit(solution)/shard_map/g1b/ppermute | solution.py:96
  82.6 9.8 %collective-permute-start.21 = (bf16[16,16,768]{2,1,0:T(8,128)(2,1)}, bf16[16,16,768]{2,1,0:T(8,128)(2,1)}, u32[]{:S(2)}, u32[]{:S(2)}) collective-permute-start(bf16[16,16,768]{2,1,0:T(8,128)(2,1)} %collective-permute-done.13.rest_0_), channel_id=1, source_target_pairs={{0,4},{1,13},{2,6},{3,15},{4,8},{5,1},{6,10},{7,3},{8,12},{9,5},{1... | collective-permute-start | bytes 1179656 | tf_op jit(solution)/shard_map/f_from3a/ppermute | solution.py:96
  84.3 15.0 %collective-permute-start.16 = (bf16[16,16,768]{2,1,0:T(8,128)(2,1)}, bf16[16,16,768]{2,1,0:T(8,128)(2,1)}, u32[]{:S(2)}, u32[]{:S(2)}) collective-permute-start(bf16[16,16,768]{2,1,0:T(8,128)(2,1)} %collective-permute-done.12.rest_1_), channel_id=1, source_target_pairs={{0,4},{1,13},{2,6},{3,15},{4,8},{5,1},{6,10},{7,3},{8,12},{9,5},{1... | collective-permute-start | bytes 1179656 | tf_op jit(solution)/shard_map/f_from3b/ppermute | solution.py:96
  89.2 8.3 %collective-permute-start.20 = (bf16[16,16,768]{2,1,0:T(8,128)(2,1)}, bf16[16,16,768]{2,1,0:T(8,128)(2,1)}, u32[]{:S(2)}, u32[]{:S(2)}) collective-permute-start(bf16[16,16,768]{2,1,0:T(8,128)(2,1)} %add_convert_fusion.1), channel_id=1, source_target_pairs={{0,16},{1,17},{2,18},{3,19},{4,20},{5,21},{6,22},{7,23},{8,24},{9,... | collective-permute-start | bytes 1179656 | tf_op jit(solution)/shard_map/g_left/ppermute | solution.py:87
  90.0 9.3 %collective-permute-start.19 = (bf16[16,16,768]{2,1,0:T(8,128)(2,1)}, bf16[16,16,768]{2,1,0:T(8,128)(2,1)}, u32[]{:S(2)}, u32[]{:S(2)}) collective-permute-start(bf16[16,16,768]{2,1,0:T(8,128)(2,1)} %add_convert_fusion), channel_id=1, source_target_pairs={{0,18},{1,19},{2,16},{3,17},{4,22},{5,23},{6,20},{7,21},{8,26},{9,... | collective-permute-start | bytes 1179656 | tf_op jit(solution)/shard_map/g_right/ppermute | solution.py:87
  92.4 12.9 %collective-permute-start.23 = (bf16[16,16,768]{2,1,0:T(8,128)(2,1)}, bf16[16,16,768]{2,1,0:T(8,128)(2,1)S(1)}, u32[]{:S(2)}, u32[]{:S(2)}) collective-permute-start(bf16[16,16,768]{2,1,0:T(8,128)(2,1)} %collective-permute-done.21.rest_6_), channel_id=1, source_target_pairs={{0,4},{1,13},{2,6},{3,15},{4,8},{5,1},{6,10},{7,3},{8,12},{9,5},{1... | collective-permute-start | bytes 1179656 | tf_op jit(solution)/shard_map/f_from2a/ppermute | solution.py:96
  99.3 20.9 %collective-permute-start.22 = (bf16[16,16,768]{2,1,0:T(8,128)(2,1)}, bf16[16,16,768]{2,1,0:T(8,128)(2,1)S(1)}, u32[]{:S(2)}, u32[]{:S(2)}) collective-permute-start(bf16[16,16,768]{2,1,0:T(8,128)(2,1)} %collective-permute-done.16.rest_7_), channel_id=1, source_target_pairs={{0,4},{1,13},{2,6},{3,15},{4,8},{5,1},{6,10},{7,3},{8,12},{9,5},{1... | collective-permute-start | bytes 1179656 | tf_op jit(solution)/shard_map/f_from2b/ppermute | solution.py:96
  105.4 18.5 %collective-permute-start.27 = (bf16[16,16,768]{2,1,0:T(8,128)(2,1)S(1)}, bf16[16,16,768]{2,1,0:T(8,128)(2,1)S(1)}, u32[]{:S(2)}, u32[]{:S(2)}) collective-permute-start(bf16[16,16,768]{2,1,0:T(8,128)(2,1)S(1)} %collective-permute-done.23.rest_4_), channel_id=1, source_target_pairs={{0,4},{1,13},{2,6},{3,15},{4,8},{5,1},{6,10},{7,3},{8,12},{9,5},{1... | collective-permute-start | bytes 1179656 | tf_op jit(solution)/shard_map/f_from1a/ppermute | solution.py:96
  107.1 18.8 %collective-permute-start.26 = (bf16[16,16,768]{2,1,0:T(8,128)(2,1)S(1)}, bf16[16,16,768]{2,1,0:T(8,128)(2,1)S(1)}, u32[]{:S(2)}, u32[]{:S(2)}) collective-permute-start(bf16[16,16,768]{2,1,0:T(8,128)(2,1)S(1)} %get-tuple-element.446), channel_id=1, source_target_pairs={{0,18},{1,19},{2,16},{3,17},{4,22},{5,23},{6,20},{7,21},{8,26},{9,... | collective-permute-start | bytes 1179656 | tf_op jit(solution)/shard_map/g_back_a/ppermute | solution.py:87
  117.0 10.3 %collective-permute-start.25 = (bf16[16,16,768]{2,1,0:T(8,128)(2,1)S(1)}, bf16[16,16,768]{2,1,0:T(8,128)(2,1)S(1)}, u32[]{:S(2)}, u32[]{:S(2)}) collective-permute-start(bf16[16,16,768]{2,1,0:T(8,128)(2,1)S(1)} %get-tuple-element.446), channel_id=1, source_target_pairs={{0,16},{1,17},{2,18},{3,19},{4,20},{5,21},{6,22},{7,23},{8,24},{9,... | collective-permute-start | bytes 1179656 | tf_op jit(solution)/shard_map/g_back_b/ppermute | solution.py:87
  120.2 9.0 %collective-permute-start.24 = (bf16[16,16,768]{2,1,0:T(8,128)(2,1)S(1)}, bf16[16,16,768]{2,1,0:T(8,128)(2,1)S(1)}, u32[]{:S(2)}, u32[]{:S(2)}) collective-permute-start(bf16[16,16,768]{2,1,0:T(8,128)(2,1)S(1)} %collective-permute-done.22.rest_5_), channel_id=1, source_target_pairs={{0,4},{1,13},{2,6},{3,15},{4,8},{5,1},{6,10},{7,3},{8,12},{9,5},{1... | collective-permute-start | bytes 1179656 | tf_op jit(solution)/shard_map/f_from1b/ppermute | solution.py:96
  125.9 9.0 %collective-permute-start.31 = (bf16[16,16,768]{2,1,0:T(8,128)(2,1)S(1)}, bf16[16,16,768]{2,1,0:T(8,128)(2,1)S(1)}, u32[]{:S(2)}, u32[]{:S(2)}) collective-permute-start(bf16[16,16,768]{2,1,0:T(8,128)(2,1)S(1)} %collective-permute-done.26.rest_0_), channel_id=1, source_target_pairs={{0,4},{1,13},{2,6},{3,15},{4,8},{5,1},{6,10},{7,3},{8,12},{9,5},{1... | collective-permute-start | bytes 1179656 | tf_op jit(solution)/shard_map/g_from3a/ppermute | solution.py:96
  127.3 11.9 %collective-permute-start.30 = (bf16[16,16,768]{2,1,0:T(8,128)(2,1)S(1)}, bf16[16,16,768]{2,1,0:T(8,128)(2,1)S(1)}, u32[]{:S(2)}, u32[]{:S(2)}) collective-permute-start(bf16[16,16,768]{2,1,0:T(8,128)(2,1)S(1)} %collective-permute-done.25.rest_1_), channel_id=1, source_target_pairs={{0,4},{1,13},{2,6},{3,15},{4,8},{5,1},{6,10},{7,3},{8,12},{9,5},{1... | collective-permute-start | bytes 1179656 | tf_op jit(solution)/shard_map/g_from3b/ppermute | solution.py:96
  134.9 9.7 %collective-permute-start.36 = (bf16[16,16,768]{2,1,0:T(8,128)(2,1)S(1)}, bf16[16,16,768]{2,1,0:T(8,128)(2,1)S(1)}, u32[]{:S(2)}, u32[]{:S(2)}) collective-permute-start(bf16[16,16,768]{2,1,0:T(8,128)(2,1)S(1)} %collective-permute-done.31.rest_6_), channel_id=1, source_target_pairs={{0,4},{1,13},{2,6},{3,15},{4,8},{5,1},{6,10},{7,3},{8,12},{9,5},{1... | collective-permute-start | bytes 1179656 | tf_op jit(solution)/shard_map/g_from2a/ppermute | solution.py:96
  135.1 4.2 %collective-permute-start.29 = (bf16[416,384]{1,0:T(8,128)(2,1)S(1)}, bf16[416,384]{1,0:T(8,128)(2,1)S(1)}, u32[]{:S(2)}, u32[]{:S(2)}) collective-permute-start(bf16[416,384]{1,0:T(8,128)(2,1)S(1)} %get-tuple-element.468), channel_id=1, source_target_pairs={{0,1},{1,0},{2,3},{3,2},{4,5},{5,4},{6,7},{7,6},{8,9},{9,8},{10,11... | collective-permute-start | bytes 958472 | tf_op jit(solution)/shard_map/sum_core/ppermute | solution.py:105
  139.1 9.0 %collective-permute-start.35 = (bf16[16,16,768]{2,1,0:T(8,128)(2,1)S(1)}, bf16[16,16,768]{2,1,0:T(8,128)(2,1)S(1)}, u32[]{:S(2)}, u32[]{:S(2)}) collective-permute-start(bf16[16,16,768]{2,1,0:T(8,128)(2,1)S(1)} %collective-permute-done.30.rest_7_), channel_id=1, source_target_pairs={{0,4},{1,13},{2,6},{3,15},{4,8},{5,1},{6,10},{7,3},{8,12},{9,5},{1... | collective-permute-start | bytes 1179656 | tf_op jit(solution)/shard_map/g_from2b/ppermute | solution.py:96
  139.9 8.3 %collective-permute-start.32 = (bf16[104,384]{1,0:T(8,128)(2,1)S(1)}, bf16[104,384]{1,0:T(8,128)(2,1)S(1)}, u32[]{:S(2)}, u32[]{:S(2)}) collective-permute-start(bf16[104,384]{1,0:T(8,128)(2,1)S(1)} %get-tuple-element.486), channel_id=1, source_target_pairs={{0,32},{1,33},{2,34},{3,35},{4,36},{5,37},{6,38},{7,39},{8,40},{9,... | collective-permute-start | bytes 239624 | tf_op jit(solution)/shard_map/sum_y/ppermute | solution.py:105
  141.5 6.6 %collective-permute-start.33 = (bf16[104,384]{1,0:T(8,128)(2,1)S(1)}, bf16[104,384]{1,0:T(8,128)(2,1)S(1)}, u32[]{:S(2)}, u32[]{:S(2)}) collective-permute-start(bf16[104,384]{1,0:T(8,128)(2,1)S(1)} %get-tuple-element.487), channel_id=1, source_target_pairs={{0,64},{1,65},{2,66},{3,67},{4,68},{5,69},{6,70},{7,71},{8,72},{9,... | collective-permute-start | bytes 239624 | tf_op jit(solution)/shard_map/sum_y/ppermute | solution.py:105
  144.4 5.6 %collective-permute-start.34 = (bf16[104,384]{1,0:T(8,128)(2,1)S(1)}, bf16[104,384]{1,0:T(8,128)(2,1)S(1)}, u32[]{:S(2)}, u32[]{:S(2)}) collective-permute-start(bf16[104,384]{1,0:T(8,128)(2,1)S(1)} %get-tuple-element.488), channel_id=1, source_target_pairs={{0,96},{1,97},{2,98},{3,99},{4,100},{5,101},{6,102},{7,103},{8,104... | collective-permute-start | bytes 239624 | tf_op jit(solution)/shard_map/sum_y/ppermute | solution.py:105
  144.7 9.0 %collective-permute-start.38 = (bf16[16,16,768]{2,1,0:T(8,128)(2,1)S(1)}, bf16[16,16,768]{2,1,0:T(8,128)(2,1)S(1)}, u32[]{:S(2)}, u32[]{:S(2)}) collective-permute-start(bf16[16,16,768]{2,1,0:T(8,128)(2,1)S(1)} %collective-permute-done.36.rest_4_), channel_id=1, source_target_pairs={{0,4},{1,13},{2,6},{3,15},{4,8},{5,1},{6,10},{7,3},{8,12},{9,5},{1... | collective-permute-start | bytes 1179656 | tf_op jit(solution)/shard_map/g_from1a/ppermute | solution.py:96
  148.1 9.7 %collective-permute-start.40 = (bf16[16,16,768]{2,1,0:T(8,128)(2,1)S(1)}, bf16[16,16,768]{2,1,0:T(8,128)(2,1)S(1)}, u32[]{:S(2)}, u32[]{:S(2)}) collective-permute-start(bf16[16,16,768]{2,1,0:T(8,128)(2,1)S(1)} %collective-permute-done.35.rest_5_), channel_id=1, source_target_pairs={{0,4},{1,13},{2,6},{3,15},{4,8},{5,1},{6,10},{7,3},{8,12},{9,5},{1... | collective-permute-start | bytes 1179656 | tf_op jit(solution)/shard_map/g_from1b/ppermute | solution.py:96
  150.1 4.5 %collective-permute-start.37 = (bf16[104,384]{1,0:T(8,128)(2,1)S(1)}, bf16[104,384]{1,0:T(8,128)(2,1)S(1)}, u32[]{:S(2)}, u32[]{:S(2)}) collective-permute-start(bf16[104,384]{1,0:T(8,128)(2,1)S(1)} %add_convert_fusion.16), channel_id=1, source_target_pairs={{0,16},{1,17},{2,18},{3,19},{4,20},{5,21},{6,22},{7,23},{8,24},{9,... | collective-permute-start | bytes 239624 | tf_op jit(solution)/shard_map/sum_x1/ppermute | solution.py:105
  150.2 24.2 %collective-permute-start.28 = (bf16[8,11,16,768]{3,2,1,0:T(8,128)(2,1)}, bf16[8,11,16,768]{3,2,1,0:T(8,128)(2,1)S(1)}, u32[]{:S(2)}, u32[]{:S(2)}) collective-permute-start(bf16[8,11,16,768]{3,2,1,0:T(8,128)(2,1)} %get-tuple-element.466), channel_id=1, source_target_pairs={{0,1},{1,0},{2,3},{3,2},{4,5},{5,4},{6,7},{7,6},{8,9},{9,8},{10,11... | collective-permute-start | bytes 6488072 | tf_op jit(solution)/shard_map/f_pair_back/ppermute | solution.py:105
  154.6 6.0 %collective-permute-start.39 = (bf16[104,384]{1,0:T(8,128)(2,1)S(1)}, bf16[104,384]{1,0:T(8,128)(2,1)S(1)}, u32[]{:S(2)}, u32[]{:S(2)}) collective-permute-start(bf16[104,384]{1,0:T(8,128)(2,1)S(1)} %add_convert_fusion.15), channel_id=1, source_target_pairs={{0,2},{1,3},{2,0},{3,1},{4,6},{5,7},{6,4},{7,5},{8,10},{9,11},{10,... | collective-permute-start | bytes 239624 | tf_op jit(solution)/shard_map/sum_x2/ppermute | solution.py:105
  165.8 21.6 %collective-permute-start.42 = (bf16[8,11,16,768]{3,2,1,0:T(8,128)(2,1)}, bf16[8,11,16,768]{3,2,1,0:T(8,128)(2,1)}, u32[]{:S(2)}, u32[]{:S(2)}) collective-permute-start(bf16[8,11,16,768]{3,2,1,0:T(8,128)(2,1)} %get-tuple-element.524), channel_id=1, source_target_pairs={{0,1},{1,0},{2,3},{3,2},{4,5},{5,4},{6,7},{7,6},{8,9},{9,8},{10,11... | collective-permute-start | bytes 6488072 | tf_op jit(solution)/shard_map/g_pair_back/ppermute | solution.py:105
  165.8 4.8 %collective-permute-start.41 = (bf16[104,384]{1,0:T(8,128)(2,1)S(1)}, bf16[104,384]{1,0:T(8,128)(2,1)S(1)}, u32[]{:S(2)}, u32[]{:S(2)}) collective-permute-start(bf16[104,384]{1,0:T(8,128)(2,1)S(1)} %add_convert_fusion.14), channel_id=1, source_target_pairs={{0,4},{1,5},{2,6},{3,7},{4,0},{5,1},{6,2},{7,3},{8,12},{9,13},{10,... | collective-permute-start | bytes 239624 | tf_op jit(solution)/shard_map/sum_z1/ppermute | solution.py:105
  170.7 10.5 %collective-permute-start.43 = (bf16[104,384]{1,0:T(8,128)(2,1)S(1)}, bf16[104,384]{1,0:T(8,128)(2,1)S(1)}, u32[]{:S(2)}, u32[]{:S(2)}) collective-permute-start(bf16[104,384]{1,0:T(8,128)(2,1)S(1)} %add_convert_fusion.13), channel_id=1, source_target_pairs={{0,8},{1,9},{2,10},{3,11},{4,12},{5,13},{6,14},{7,15},{8,0},{9,1},... | collective-permute-start | bytes 239624 | tf_op jit(solution)/shard_map/sum_z2/ppermute | solution.py:105
  181.2 1.4 collective-permute-start.44
  182.6 15.6 %collective-permute-start.45 = (bf16[2,104,384]{2,1,0:T(8,128)(2,1)S(1)}, bf16[2,104,384]{2,1,0:T(8,128)(2,1)S(1)}, u32[]{:S(2)}, u32[]{:S(2)}) collective-permute-start(bf16[2,104,384]{2,1,0:T(8,128)(2,1)S(1)} %pad_maximum_fusion.p0), channel_id=1, source_target_pairs={{0,32},{1,33},{2,34},{3,35},{4,36},{5,37},{6,38},{7,39},{8,40},{9,... | collective-permute-start | bytes 479240 | tf_op jit(solution)/shard_map/all_y/ppermute | solution.py:105
  182.7 15.5 %collective-permute-start.46 = (bf16[2,104,384]{2,1,0:T(8,128)(2,1)S(1)}, bf16[2,104,384]{2,1,0:T(8,128)(2,1)S(1)}, u32[]{:S(2)}, u32[]{:S(2)}) collective-permute-start(bf16[2,104,384]{2,1,0:T(8,128)(2,1)S(1)} %pad_maximum_fusion.p0), channel_id=1, source_target_pairs={{0,64},{1,65},{2,66},{3,67},{4,68},{5,69},{6,70},{7,71},{8,72},{9,... | collective-permute-start | bytes 479240 | tf_op jit(solution)/shard_map/all_y/ppermute | solution.py:105
  185.3 12.9 %collective-permute-start.47 = (bf16[2,104,384]{2,1,0:T(8,128)(2,1)S(1)}, bf16[2,104,384]{2,1,0:T(8,128)(2,1)S(1)}, u32[]{:S(2)}, u32[]{:S(2)}) collective-permute-start(bf16[2,104,384]{2,1,0:T(8,128)(2,1)S(1)} %pad_maximum_fusion.p0), channel_id=1, source_target_pairs={{0,96},{1,97},{2,98},{3,99},{4,100},{5,101},{6,102},{7,103},{8,104... | collective-permute-start | bytes 479240 | tf_op jit(solution)/shard_map/all_y/ppermute | solution.py:105
  (27 other events, 374.2 us)
